TPU v7x, 32 devices: a whole 2x2x4 slice. The times are simulated.
32 devices in a mesh: rep: 4 (over x, core), shard: 8 (over z, y).
Axes of the slice: x: 2, y: 2, z: 4, core: 2. Of those that a mesh axis runs over, the one named last changes fastest.
Arguments:
- hidden_acts: bfloat16 [24576, 128], P(('rep', 'shard')), may hold values from -6 to 6
- out_cotangent: bfloat16 [24576, 4096], P(('rep', 'shard')), may hold values from -0.0390625 to 0.0390625
- weight: bfloat16 [128, 4096], P('shard'), may hold values from -6 to 6
- first_moment: float32 [128, 4096], P('shard'), may hold values from -6 to 6
- second_moment: float32 [128, 4096], P('shard'), may hold values from 0.05 to 2
Outputs:
- new_weight: bfloat16 [128, 4096], replicated
- new_first: float32 [128, 4096], P('shard')
- new_second: float32 [128, 4096], P('shard')
All inputs are finite; a program needn't handle non-finite values.
Results may differ from a plain program's by a relative error of at most 0.0014.
Values may be sent and summed in bfloat16 or wider, within the bound.
No kernel may reach another device: no remote copies, remote signals or barrier semaphores. Data moves between devices by JAX's collectives and lax.ppermute only.
A program may use at most 128 MiB of HBM per device.

v0:
```python
import functools

import jax
import jax.numpy as jnp
from jax import lax
from jax.experimental import pallas as pl
from jax.experimental.pallas import tpu as pltpu
from jax.sharding import PartitionSpec as P

F32 = jnp.float32
BF16 = jnp.bfloat16
CHUNK = 512
LOAD_LIMIT = 48 * 1024 * 1024


def adamw_moments(first_moment, second_moment, grad):
    new_first = 0.9 * first_moment + 0.1 * grad
    new_second = 0.999 * second_moment + 0.001 * grad * grad
    return new_first, new_second


def adamw_weight(weight, new_first, new_second):
    corr_one = 0.9999734386011124
    corr_two = 0.0952078528
    wfloat = weight.astype(F32)
    update = new_first / corr_one / (jnp.sqrt(new_second / corr_two) + 1e-08)
    return (wfloat - 0.05 * (update + 0.1 * wfloat)).astype(BF16)


def shape(dims, kind):
    return jax.ShapeDtypeStruct(dims, kind)


def call(kernel, outs, *args, far_in=(), far_out=0, scratch=(), aliases=None, limit=48 * 1024 * 1024):
    near, far = pl.BlockSpec(memory_space=pltpu.VMEM), pl.BlockSpec(memory_space=pltpu.HBM)
    return pl.pallas_call(
        kernel,
        out_shape=outs,
        in_specs=[far if i in far_in else near for i in range(len(args))],
        out_specs=[far if i < far_out else near for i in range(len(outs))],
        scratch_shapes=scratch,
        input_output_aliases=aliases or {},
        compiler_params=pltpu.CompilerParams(vmem_limit_bytes=limit),
    )(*args)


def exchange(value, other):
    reps, shards = lax.axis_size("rep"), lax.axis_size("shard")
    pairs = []
    for rep in range(reps):
        for shard in range(shards):
            to_rep, to_shard = other(rep, shard)
            pairs.append((rep * shards + shard, to_rep * shards + to_shard))
    return lax.ppermute(value, ("rep", "shard"), pairs)


def to_sibling(value):
    return exchange(value, lambda rep, shard: (rep ^ 1, shard))


def across(value, dy, dx):
    return exchange(value, lambda rep, shard: (rep ^ (2 * dx), shard ^ dy))


def along_z(value, k):
    return exchange(value, lambda rep, shard: (rep, shard ^ (2 * k)))


SQUARE = ((1, 1), (0, 1), (1, 0))


def far_first(levels):
    return [k for k in range(levels - 1, 0, -1)]


def place():
    rep, shard = lax.axis_index("rep"), lax.axis_index("shard")
    return rep & 1, rep >> 1, shard & 1, shard >> 1


def block(index, size):
    return pl.ds(pl.multiple_of(index * size, size), size)


def load_kernel(acts_ref, cots_ref, out, turned, kept_cots, acts, cots, sems):
    core = place()[0]
    count = cots.shape[0]
    copies = [pltpu.make_async_copy(acts_ref, acts, sems.at[count])]
    for i in range(count):
        source = cots_ref.at[:, block((1 - core) * count + i, CHUNK)]
        copies.append(pltpu.make_async_copy(source, cots.at[i], sems.at[i]))
    own = cots_ref.at[:, block(core, kept_cots.shape[1])]
    copies.append(pltpu.make_async_copy(own, kept_cots, sems.at[count + 1]))
    for copy in copies:
        copy.start()
    copies[0].wait()
    turned[...] = acts[...].T
    for i in range(count):
        copies[i + 1].wait()
        term = jnp.dot(turned[...], cots[i], preferred_element_type=F32)
        out[:, i * CHUNK:(i + 1) * CHUNK] = term.astype(out.dtype)
    copies[-1].wait()


def product_kernel(turned, cots, out):
    for i in range(out.shape[1] // CHUNK):
        at = slice(i * CHUNK, (i + 1) * CHUNK)
        out[:, at] = jnp.dot(turned[...], cots[:, at], preferred_element_type=F32)


def square_kernel(kept, came, own, *pieces):
    _, x, y, _ = place()
    some_rows, quarter = own.shape
    rows = kept.shape[0] // lax.axis_size("shard")
    for (dy, dx), out in zip(((0, 0),) + SQUARE, (own,) + pieces):
        cols = block(x ^ dx, quarter)
        for z in range(some_rows // rows):
            at = block(2 * z + (y ^ dy), rows)
            out[z * rows:(z + 1) * rows, :] = (kept[at, cols] + came[at, cols].astype(F32)).astype(out.dtype)


def line_kernel(steps, kept, *refs):
    came, (own, *pieces) = refs[:len(SQUARE)], refs[len(SQUARE):]
    z = place()[3]
    rows = own.shape[0]
    for k, out in zip([0] + steps, [own] + pieces):
        at = block(z ^ k, rows)
        total = kept[at, :]
        for ref in came:
            total += ref[at, :].astype(F32)
        out[...] = total.astype(out.dtype)


def update_kernel(w, m, v, own, *refs):
    pieces, (new_w, grad) = refs[:-2], refs[-2:]
    core, x, _, _ = place()
    total = own[...]
    for ref in pieces:
        total += ref[...].astype(F32)
    grad[...] = total.astype(BF16)
    at = block(core * 2 + x, total.shape[1])
    new_m, new_v = adamw_moments(m[:, at], v[:, at], total)
    new_w[...] = adamw_weight(w[:, at], new_m, new_v)


def pack_kernel(steps, grad, *refs):
    pieces, (out, with_grad) = refs[:-2], refs[-2:]
    z = place()[3]
    rows, some_rows = grad.shape[0], out.shape[0]
    for k, ref in zip([0] + steps, pieces):
        at = block(z ^ k, rows)
        out[at, :] = ref[...]
        with_grad[at, :] = ref[...]
    with_grad[some_rows:, :] = grad[...]


def half_kernel(own, *refs):
    parts, out = (own,) + refs[:-1], refs[-1]
    _, x, y, _ = place()
    rows = out.shape[0] // (lax.axis_size("shard") + 1)
    some_rows, quarter = parts[-1].shape
    for (dy, dx), ref in zip(((0, 0),) + SQUARE[::-1], parts):
        cols = block(x ^ dx, quarter)
        for z in range(some_rows // rows):
            out[block(2 * z + (y ^ dy), rows), cols] = ref[z * rows:(z + 1) * rows, :]
        if dy == 0:
            out[2 * some_rows:, cols] = ref[some_rows:, :]


def write_kernel(away, part, m, v, *refs):
    w_out, m_out, v_out, new_m, new_v, sems = refs[-6:]
    core = place()[0]
    all_rows, half = w_out.shape[0], part.shape[1]
    at = block(1 - core if away else core, half)
    copies = [pltpu.make_async_copy(part.at[pl.ds(0, all_rows), :], w_out.at[:, at], sems.at[0])]
    copies[0].start()
    new_m[...], new_v[...] = adamw_moments(m[:, at], v[:, at], part[all_rows:, :].astype(F32))
    for i, (source, out) in enumerate(((new_m, m_out), (new_v, v_out))):
        copies.append(pltpu.make_async_copy(source, out.at[:, at], sems.at[i + 1]))
        copies[-1].start()
    for copy in copies:
        copy.wait()


def body(hidden_acts, out_cotangent, weight, first_moment, second_moment):
    rows, width = weight.shape
    tokens, all_rows = hidden_acts.shape
    some_rows, levels = all_rows // 2, lax.axis_size("shard") // 2
    half, quarter = width // 2, width // 4
    count = half // CHUNK
    steps = far_first(levels)

    away, turned, cots = call(
        load_kernel,
        [shape((all_rows, half), BF16), shape((all_rows, tokens), BF16), shape((tokens, half), BF16)],
        hidden_acts, out_cotangent, far_in=(0, 1),
        scratch=[
            pltpu.VMEM((tokens, all_rows), BF16),
            pltpu.VMEM((count, tokens, CHUNK), BF16),
            pltpu.SemaphoreType.DMA((count + 2,)),
        ],
        limit=LOAD_LIMIT,
    )
    came = to_sibling(away)
    kept = call(product_kernel, [shape((all_rows, half), F32)], turned, cots)[0]

    own, *pieces = call(
        square_kernel,
        [shape((some_rows, quarter), F32)] + [shape((some_rows, quarter), BF16)] * len(SQUARE), kept, came,
    )
    came = [across(piece, *step) for step, piece in zip(SQUARE, pieces)]
    own, *pieces = call(
        functools.partial(line_kernel, steps),
        [shape((rows, quarter), F32)] + [shape((rows, quarter), BF16)] * (levels - 1), own, *came,
    )
    pieces = [along_z(piece, k) for k, piece in zip(steps, pieces)]
    new_w, grad = call(
        update_kernel, [shape((rows, quarter), BF16)] * 2,
        weight, first_moment, second_moment, own, *pieces,
    )

    back = steps[::-1]
    pieces = [new_w] + [along_z(new_w, k) for k in back]
    mine, with_grad = call(
        functools.partial(pack_kernel, back),
        [shape((some_rows, quarter), BF16), shape((some_rows + rows, quarter), BF16)], grad, *pieces,
    )
    parts = [across(mine if dy else with_grad, dy, dx) for dy, dx in SQUARE[::-1]]
    part = call(half_kernel, [shape((all_rows + rows, half), BF16)], with_grad, *parts)[0]
    other = to_sibling(part)
    results = [shape((all_rows, width), BF16), shape((rows, width), F32), shape((rows, width), F32)]
    scratch = [pltpu.VMEM((rows, half), F32), pltpu.VMEM((rows, half), F32), pltpu.SemaphoreType.DMA((3,))]
    written = call(
        functools.partial(write_kernel, False), results,
        part, first_moment, second_moment, far_out=3, scratch=scratch,
    )
    return tuple(call(
        functools.partial(write_kernel, True), results,
        other, first_moment, second_moment, *written,
        far_in=(3, 4, 5), far_out=3, scratch=scratch, aliases={3: 0, 4: 1, 5: 2},
    ))


def solution(mesh):
    return jax.shard_map(
        body,
        mesh=mesh,
        in_specs=(
            P(("rep", "shard"), None),
            P(("rep", "shard"), None),
            P("shard", None),
            P("shard", None),
            P("shard", None),
        ),
        out_specs=(P(), P("shard", None), P("shard", None)),
        check_vma=False,
    )
```

profile of v0, /device:TPU:0, one launch (start us, length us, event | category | flops | bytes accessed | tf_op | source)
XLA Modules:
  0.0 45.4 jit_solution(5100325605517214663)
XLA Ops:
  0.7 1.0 %copy-done.2 = bf16[768,128]{1,0:T(8,128)(2,1)S(1)} copy-done((bf16[768,128]{1,0:T(8,128)(2,1)S(1)}, bf16[768,128]{1,0:T(8,128)(2,1)}, u32[]{:S(2)}) %copy-start.2) | copy-done | bytes 196632
  1.6 3.2 %shard_map.76 = (bf16[128,2048]{1,0:T(8,128)(2,1)S(1)}, bf16[128,768]{1,0:T(8,128)(2,1)S(1)}, bf16[768,2048]{1,0:T(8,128)(2,1)S(1)}) custom-call(bf16[768,128]{1,0:T(8,128)(2,1)S(1)} %copy-done.2, bf16[768,4096]{1,0:T(8,128)(2,1)} %cots_ref.1), custom_call_target="tpu_custom_call" | custom-call | tf_op jit(solution)/shard_map/pallas_call | solution.py:36
  5.3 0.6 %shard_map.77.kept = f32[128,2048]{1,0:T(8,128)S(1)} custom-call(bf16[128,768]{1,0:T(8,128)(2,1)S(1)} %get-tuple-element.21.turned, bf16[768,2048]{1,0:T(8,128)(2,1)S(1)} %get-tuple-element.22.cots), custom_call_target="tpu_custom_call" | custom-call | tf_op jit(solution)/shard_map/pallas_call | solution.py:36
  5.9 1.0 %collective-permute-done.came = bf16[128,2048]{1,0:T(8,128)(2,1)S(1)} collective-permute-done((bf16[128,2048]{1,0:T(8,128)(2,1)S(1)}, bf16[128,2048]{1,0:T(8,128)(2,1)S(1)}, u32[]{:S(2)}, u32[]{:S(2)}) %collective-permute-start) | collective-permute-done | bytes 524320 | tf_op jit(solution)/shard_map/ppermute | solution.py:54
  7.0 3.9 %collective-permute-start.1 = (bf16[64,1024]{1,0:T(8,128)(2,1)S(1)}, bf16[64,1024]{1,0:T(8,128)(2,1)S(1)}, u32[]{:S(2)}, u32[]{:S(2)}) collective-permute-start(bf16[64,1024]{1,0:T(8,128)(2,1)S(1)} %get-tuple-element.25), channel_id=1, source_target_pairs={{0,17},{1,16},{2,19},{3,18},{4,21},{5,20},{6,23},{7,22},{8,25},{9,... | collective-permute-start | bytes 393224 | tf_op jit(solution)/shard_map/ppermute | solution.py:54
  11.5 3.6 %collective-permute-done.1.refs_0_ = bf16[64,1024]{1,0:T(8,128)(2,1)S(1)} collective-permute-done((bf16[64,1024]{1,0:T(8,128)(2,1)S(1)}, bf16[64,1024]{1,0:T(8,128)(2,1)S(1)}, u32[]{:S(2)}, u32[]{:S(2)}) %collective-permute-start.1) | collective-permute-done | bytes 131104 | tf_op jit(solution)/shard_map/ppermute | solution.py:54
  15.1 2.6 %collective-permute-done.2.refs_1_ = bf16[64,1024]{1,0:T(8,128)(2,1)S(1)} collective-permute-done((bf16[64,1024]{1,0:T(8,128)(2,1)S(1)}, bf16[64,1024]{1,0:T(8,128)(2,1)S(1)}, u32[]{:S(2)}, u32[]{:S(2)}) %collective-permute-start.2) | collective-permute-done | bytes 131104 | tf_op jit(solution)/shard_map/ppermute | solution.py:54
  17.8 3.7 %collective-permute-start.4 = (bf16[16,1024]{1,0:T(8,128)(2,1)S(1)}, bf16[16,1024]{1,0:T(8,128)(2,1)S(1)}, u32[]{:S(2)}, u32[]{:S(2)}) collective-permute-start(bf16[16,1024]{1,0:T(8,128)(2,1)S(1)} %get-tuple-element.29), channel_id=1, source_target_pairs={{0,6},{1,7},{2,4},{3,5},{4,2},{5,3},{6,0},{7,1},{8,14},{9,15},{10,... | collective-permute-start | bytes 98312 | tf_op jit(solution)/shard_map/ppermute | solution.py:54
  21.4 0.8 %collective-permute-start.6 = (bf16[16,1024]{1,0:T(8,128)(2,1)S(1)}, bf16[16,1024]{1,0:T(8,128)(2,1)S(1)}, u32[]{:S(2)}, u32[]{:S(2)}) collective-permute-start(bf16[16,1024]{1,0:T(8,128)(2,1)S(1)} %get-tuple-element.31), channel_id=1, source_target_pairs={{0,2},{1,3},{2,0},{3,1},{4,6},{5,7},{6,4},{7,5},{8,10},{9,11},{10,... | collective-permute-start | bytes 98312 | tf_op jit(solution)/shard_map/ppermute | solution.py:54
  22.2 1.7 %collective-permute-done.4.refs_0_ = bf16[16,1024]{1,0:T(8,128)(2,1)S(1)} collective-permute-done((bf16[16,1024]{1,0:T(8,128)(2,1)S(1)}, bf16[16,1024]{1,0:T(8,128)(2,1)S(1)}, u32[]{:S(2)}, u32[]{:S(2)}) %collective-permute-start.4) | collective-permute-done | bytes 32800 | tf_op jit(solution)/shard_map/ppermute | solution.py:54
  23.9 2.3 %collective-permute-done.5.refs_1_ = bf16[16,1024]{1,0:T(8,128)(2,1)S(1)} collective-permute-done((bf16[16,1024]{1,0:T(8,128)(2,1)S(1)}, bf16[16,1024]{1,0:T(8,128)(2,1)S(1)}, u32[]{:S(2)}, u32[]{:S(2)}) %collective-permute-start.5) | collective-permute-done | bytes 32800 | tf_op jit(solution)/shard_map/ppermute | solution.py:54
  26.3 1.5 %collective-permute-start.9 = (bf16[16,1024]{1,0:T(8,128)(2,1)S(1)}, bf16[16,1024]{1,0:T(8,128)(2,1)S(1)}, u32[]{:S(2)}, u32[]{:S(2)}) collective-permute-start(bf16[16,1024]{1,0:T(8,128)(2,1)S(1)} %get-tuple-element.33.refs_0_), channel_id=1, source_target_pairs={{0,6},{1,7},{2,4},{3,5},{4,2},{5,3},{6,0},{7,1},{8,14},{9,15},{10,... | collective-permute-start | bytes 98312 | tf_op jit(solution)/shard_map/ppermute | solution.py:54
  27.9 0.6 %collective-permute-start.8 = (bf16[16,1024]{1,0:T(8,128)(2,1)S(1)}, bf16[16,1024]{1,0:T(8,128)(2,1)S(1)}, u32[]{:S(2)}, u32[]{:S(2)}) collective-permute-start(bf16[16,1024]{1,0:T(8,128)(2,1)S(1)} %get-tuple-element.33.refs_0_), channel_id=1, source_target_pairs={{0,4},{1,5},{2,6},{3,7},{4,0},{5,1},{6,2},{7,3},{8,12},{9,13},{10,... | collective-permute-start | bytes 98312 | tf_op jit(solution)/shard_map/ppermute | solution.py:54
  28.5 2.3 %collective-permute-start.7 = (bf16[16,1024]{1,0:T(8,128)(2,1)S(1)}, bf16[16,1024]{1,0:T(8,128)(2,1)S(1)}, u32[]{:S(2)}, u32[]{:S(2)}) collective-permute-start(bf16[16,1024]{1,0:T(8,128)(2,1)S(1)} %get-tuple-element.33.refs_0_), channel_id=1, source_target_pairs={{0,2},{1,3},{2,0},{3,1},{4,6},{5,7},{6,4},{7,5},{8,10},{9,11},{10,... | collective-permute-start | bytes 98312 | tf_op jit(solution)/shard_map/ppermute | solution.py:54
  30.8 1.3 %collective-permute-done.9.refs_3_ = bf16[16,1024]{1,0:T(8,128)(2,1)S(1)} collective-permute-done((bf16[16,1024]{1,0:T(8,128)(2,1)S(1)}, bf16[16,1024]{1,0:T(8,128)(2,1)S(1)}, u32[]{:S(2)}, u32[]{:S(2)}) %collective-permute-start.9) | collective-permute-done | bytes 32800 | tf_op jit(solution)/shard_map/ppermute | solution.py:54
  32.1 0.6 %collective-permute-done.8.refs_2_ = bf16[16,1024]{1,0:T(8,128)(2,1)S(1)} collective-permute-done((bf16[16,1024]{1,0:T(8,128)(2,1)S(1)}, bf16[16,1024]{1,0:T(8,128)(2,1)S(1)}, u32[]{:S(2)}, u32[]{:S(2)}) %collective-permute-start.8) | collective-permute-done | bytes 32800 | tf_op jit(solution)/shard_map/ppermute | solution.py:54
  33.1 1.6 %collective-permute-start.11 = (bf16[80,1024]{1,0:T(8,128)(2,1)S(1)}, bf16[80,1024]{1,0:T(8,128)(2,1)S(1)}, u32[]{:S(2)}, u32[]{:S(2)}) collective-permute-start(bf16[80,1024]{1,0:T(8,128)(2,1)S(1)} %get-tuple-element.34.own), channel_id=1, source_target_pairs={{0,16},{1,17},{2,18},{3,19},{4,20},{5,21},{6,22},{7,23},{8,24},{9,... | collective-permute-start | bytes 491528 | tf_op jit(solution)/shard_map/ppermute | solution.py:54
  34.6 1.4 %collective-permute-start.12 = (bf16[64,1024]{1,0:T(8,128)(2,1)S(1)}, bf16[64,1024]{1,0:T(8,128)(2,1)S(1)}, u32[]{:S(2)}, u32[]{:S(2)}) collective-permute-start(bf16[64,1024]{1,0:T(8,128)(2,1)S(1)} %get-tuple-element.35), channel_id=1, source_target_pairs={{0,17},{1,16},{2,19},{3,18},{4,21},{5,20},{6,23},{7,22},{8,25},{9,... | collective-permute-start | bytes 393224 | tf_op jit(solution)/shard_map/ppermute | solution.py:54
  36.1 0.6 %collective-permute-start.10 = (bf16[64,1024]{1,0:T(8,128)(2,1)S(1)}, bf16[64,1024]{1,0:T(8,128)(2,1)S(1)}, u32[]{:S(2)}, u32[]{:S(2)}) collective-permute-start(bf16[64,1024]{1,0:T(8,128)(2,1)S(1)} %get-tuple-element.35), channel_id=1, source_target_pairs={{0,1},{1,0},{2,3},{3,2},{4,5},{5,4},{6,7},{7,6},{8,9},{9,8},{10,11... | collective-permute-start | bytes 393224 | tf_op jit(solution)/shard_map/ppermute | solution.py:54
  36.6 4.4 %collective-permute-done.12.refs_2_ = bf16[64,1024]{1,0:T(8,128)(2,1)S(1)} collective-permute-done((bf16[64,1024]{1,0:T(8,128)(2,1)S(1)}, bf16[64,1024]{1,0:T(8,128)(2,1)S(1)}, u32[]{:S(2)}, u32[]{:S(2)}) %collective-permute-start.12) | collective-permute-done | bytes 131104 | tf_op jit(solution)/shard_map/ppermute | solution.py:54
  41.0 1.3 %collective-permute-done.10.refs_0_ = bf16[64,1024]{1,0:T(8,128)(2,1)S(1)} collective-permute-done((bf16[64,1024]{1,0:T(8,128)(2,1)S(1)}, bf16[64,1024]{1,0:T(8,128)(2,1)S(1)}, u32[]{:S(2)}, u32[]{:S(2)}) %collective-permute-start.10) | collective-permute-done | bytes 131104 | tf_op jit(solution)/shard_map/ppermute | solution.py:54
  42.5 0.9 %shard_map.83 = (bf16[128,4096]{1,0:T(8,128)(2,1)}, f32[16,4096]{1,0:T(8,128)}, f32[16,4096]{1,0:T(8,128)}) custom-call(bf16[144,2048]{1,0:T(8,128)(2,1)S(1)} %shard_map.82.part, f32[16,4096]{1,0:T(8,128)S(1)} %copy-done, f32[16,4096]{1,0:T(8,128)S(1)} %copy-done.1), custom_call_target="tpu_custom_call" | custom-call | tf_op jit(solution)/shard_map/pallas_call | solution.py:36
  43.4 1.1 %collective-permute-done.13.part = bf16[144,2048]{1,0:T(8,128)(2,1)S(1)} collective-permute-done((bf16[144,2048]{1,0:T(8,128)(2,1)S(1)}, bf16[144,2048]{1,0:T(8,128)(2,1)S(1)}, u32[]{:S(2)}, u32[]{:S(2)}) %collective-permute-start.13) | collective-permute-done | bytes 589856 | tf_op jit(solution)/shard_map/ppermute | solution.py:54
  44.5 0.9 %shard_map.84 = (bf16[128,4096]{1,0:T(8,128)(2,1)}, f32[16,4096]{1,0:T(8,128)}, f32[16,4096]{1,0:T(8,128)}) custom-call(bf16[144,2048]{1,0:T(8,128)(2,1)S(1)} %collective-permute-done.13.part, f32[16,4096]{1,0:T(8,128)S(1)} %copy-done, f32[16,4096]{1,0:T(8,128)S(1)} %copy-done.1, ...), custom_call_target="tpu_custom_call", output_to_operand_aliasing={{0}: (3, {}), {1}: (4, {}), {2}: (5, {})} | custom-call | tf_op jit(solution)/shard_map/pallas_call | solution.py:36
  (21 shorter events, 1.9 us)
Async XLA Ops:
  0.6 25.6 %copy-start.1 = (f32[16,4096]{1,0:T(8,128)S(1)}, f32[16,4096]{1,0:T(8,128)}, u32[]{:S(2)}) copy-start(f32[16,4096]{1,0:T(8,128)} %v.5) | copy-start | bytes 786436
  0.6 25.6 %copy-start = (f32[16,4096]{1,0:T(8,128)S(1)}, f32[16,4096]{1,0:T(8,128)}, u32[]{:S(2)}) copy-start(f32[16,4096]{1,0:T(8,128)} %m.5) | copy-start | bytes 786436
  0.7 1.0 %copy-start.2 = (bf16[768,128]{1,0:T(8,128)(2,1)S(1)}, bf16[768,128]{1,0:T(8,128)(2,1)}, u32[]{:S(2)}) copy-start(bf16[768,128]{1,0:T(8,128)(2,1)} %acts_ref.1) | copy-start | bytes 589828
  1.6 24.6 %copy-start.3 = (bf16[16,4096]{1,0:T(8,128)(2,1)S(1)}, bf16[16,4096]{1,0:T(8,128)(2,1)}, u32[]{:S(2)}) copy-start(bf16[16,4096]{1,0:T(8,128)(2,1)} %w.1) | copy-start | bytes 393220
  4.8 2.1 %collective-permute-start = (bf16[128,2048]{1,0:T(8,128)(2,1)S(1)}, bf16[128,2048]{1,0:T(8,128)(2,1)S(1)}, u32[]{:S(2)}, u32[]{:S(2)}) collective-permute-start(bf16[128,2048]{1,0:T(8,128)(2,1)S(1)} %get-tuple-element.23), channel_id=1, source_target_pairs={{0,8},{1,9},{2,10},{3,11},{4,12},{5,13},{6,14},{7,15},{8,0},{9,1},... | collective-permute-start | bytes 1572872 | tf_op jit(solution)/shard_map/ppermute | solution.py:54
  7.0 8.2 %collective-permute-start.1 = (bf16[64,1024]{1,0:T(8,128)(2,1)S(1)}, bf16[64,1024]{1,0:T(8,128)(2,1)S(1)}, u32[]{:S(2)}, u32[]{:S(2)}) collective-permute-start(bf16[64,1024]{1,0:T(8,128)(2,1)S(1)} %get-tuple-element.25), channel_id=1, source_target_pairs={{0,17},{1,16},{2,19},{3,18},{4,21},{5,20},{6,23},{7,22},{8,25},{9,... | collective-permute-start | bytes 393224 | tf_op jit(solution)/shard_map/ppermute | solution.py:54
  10.8 6.9 %collective-permute-start.2 = (bf16[64,1024]{1,0:T(8,128)(2,1)S(1)}, bf16[64,1024]{1,0:T(8,128)(2,1)S(1)}, u32[]{:S(2)}, u32[]{:S(2)}) collective-permute-start(bf16[64,1024]{1,0:T(8,128)(2,1)S(1)} %get-tuple-element.26), channel_id=1, source_target_pairs={{0,16},{1,17},{2,18},{3,19},{4,20},{5,21},{6,22},{7,23},{8,24},{9,... | collective-permute-start | bytes 393224 | tf_op jit(solution)/shard_map/ppermute | solution.py:54
  11.4 6.3 %collective-permute-start.3 = (bf16[64,1024]{1,0:T(8,128)(2,1)S(1)}, bf16[64,1024]{1,0:T(8,128)(2,1)S(1)}, u32[]{:S(2)}, u32[]{:S(2)}) collective-permute-start(bf16[64,1024]{1,0:T(8,128)(2,1)S(1)} %get-tuple-element.27), channel_id=1, source_target_pairs={{0,1},{1,0},{2,3},{3,2},{4,5},{5,4},{6,7},{7,6},{8,9},{9,8},{10,11... | collective-permute-start | bytes 393224 | tf_op jit(solution)/shard_map/ppermute | solution.py:54
  17.8 6.2 %collective-permute-start.4 = (bf16[16,1024]{1,0:T(8,128)(2,1)S(1)}, bf16[16,1024]{1,0:T(8,128)(2,1)S(1)}, u32[]{:S(2)}, u32[]{:S(2)}) collective-permute-start(bf16[16,1024]{1,0:T(8,128)(2,1)S(1)} %get-tuple-element.29), channel_id=1, source_target_pairs={{0,6},{1,7},{2,4},{3,5},{4,2},{5,3},{6,0},{7,1},{8,14},{9,15},{10,... | collective-permute-start | bytes 98312 | tf_op jit(solution)/shard_map/ppermute | solution.py:54
  21.4 4.8 %collective-permute-start.5 = (bf16[16,1024]{1,0:T(8,128)(2,1)S(1)}, bf16[16,1024]{1,0:T(8,128)(2,1)S(1)}, u32[]{:S(2)}, u32[]{:S(2)}) collective-permute-start(bf16[16,1024]{1,0:T(8,128)(2,1)S(1)} %get-tuple-element.30), channel_id=1, source_target_pairs={{0,4},{1,5},{2,6},{3,7},{4,0},{5,1},{6,2},{7,3},{8,12},{9,13},{10,... | collective-permute-start | bytes 98312 | tf_op jit(solution)/shard_map/ppermute | solution.py:54
  21.4 4.8 %collective-permute-start.6 = (bf16[16,1024]{1,0:T(8,128)(2,1)S(1)}, bf16[16,1024]{1,0:T(8,128)(2,1)S(1)}, u32[]{:S(2)}, u32[]{:S(2)}) collective-permute-start(bf16[16,1024]{1,0:T(8,128)(2,1)S(1)} %get-tuple-element.31), channel_id=1, source_target_pairs={{0,2},{1,3},{2,0},{3,1},{4,6},{5,7},{6,4},{7,5},{8,10},{9,11},{10,... | collective-permute-start | bytes 98312 | tf_op jit(solution)/shard_map/ppermute | solution.py:54
  26.3 5.8 %collective-permute-start.9 = (bf16[16,1024]{1,0:T(8,128)(2,1)S(1)}, bf16[16,1024]{1,0:T(8,128)(2,1)S(1)}, u32[]{:S(2)}, u32[]{:S(2)}) collective-permute-start(bf16[16,1024]{1,0:T(8,128)(2,1)S(1)} %get-tuple-element.33.refs_0_), channel_id=1, source_target_pairs={{0,6},{1,7},{2,4},{3,5},{4,2},{5,3},{6,0},{7,1},{8,14},{9,15},{10,... | collective-permute-start | bytes 98312 | tf_op jit(solution)/shard_map/ppermute | solution.py:54
  27.9 4.8 %collective-permute-start.8 = (bf16[16,1024]{1,0:T(8,128)(2,1)S(1)}, bf16[16,1024]{1,0:T(8,128)(2,1)S(1)}, u32[]{:S(2)}, u32[]{:S(2)}) collective-permute-start(bf16[16,1024]{1,0:T(8,128)(2,1)S(1)} %get-tuple-element.33.refs_0_), channel_id=1, source_target_pairs={{0,4},{1,5},{2,6},{3,7},{4,0},{5,1},{6,2},{7,3},{8,12},{9,13},{10,... | collective-permute-start | bytes 98312 | tf_op jit(solution)/shard_map/ppermute | solution.py:54
  28.5 4.5 %collective-permute-start.7 = (bf16[16,1024]{1,0:T(8,128)(2,1)S(1)}, bf16[16,1024]{1,0:T(8,128)(2,1)S(1)}, u32[]{:S(2)}, u32[]{:S(2)}) collective-permute-start(bf16[16,1024]{1,0:T(8,128)(2,1)S(1)} %get-tuple-element.33.refs_0_), channel_id=1, source_target_pairs={{0,2},{1,3},{2,0},{3,1},{4,6},{5,7},{6,4},{7,5},{8,10},{9,11},{10,... | collective-permute-start | bytes 98312 | tf_op jit(solution)/shard_map/ppermute | solution.py:54
  33.1 9.3 %collective-permute-start.11 = (bf16[80,1024]{1,0:T(8,128)(2,1)S(1)}, bf16[80,1024]{1,0:T(8,128)(2,1)S(1)}, u32[]{:S(2)}, u32[]{:S(2)}) collective-permute-start(bf16[80,1024]{1,0:T(8,128)(2,1)S(1)} %get-tuple-element.34.own), channel_id=1, source_target_pairs={{0,16},{1,17},{2,18},{3,19},{4,20},{5,21},{6,22},{7,23},{8,24},{9,... | collective-permute-start | bytes 491528 | tf_op jit(solution)/shard_map/ppermute | solution.py:54
  34.6 6.4 %collective-permute-start.12 = (bf16[64,1024]{1,0:T(8,128)(2,1)S(1)}, bf16[64,1024]{1,0:T(8,128)(2,1)S(1)}, u32[]{:S(2)}, u32[]{:S(2)}) collective-permute-start(bf16[64,1024]{1,0:T(8,128)(2,1)S(1)} %get-tuple-element.35), channel_id=1, source_target_pairs={{0,17},{1,16},{2,19},{3,18},{4,21},{5,20},{6,23},{7,22},{8,25},{9,... | collective-permute-start | bytes 393224 | tf_op jit(solution)/shard_map/ppermute | solution.py:54
  36.1 6.3 %collective-permute-start.10 = (bf16[64,1024]{1,0:T(8,128)(2,1)S(1)}, bf16[64,1024]{1,0:T(8,128)(2,1)S(1)}, u32[]{:S(2)}, u32[]{:S(2)}) collective-permute-start(bf16[64,1024]{1,0:T(8,128)(2,1)S(1)} %get-tuple-element.35), channel_id=1, source_target_pairs={{0,1},{1,0},{2,3},{3,2},{4,5},{5,4},{6,7},{7,6},{8,9},{9,8},{10,11... | collective-permute-start | bytes 393224 | tf_op jit(solution)/shard_map/ppermute | solution.py:54
  42.4 2.1 %collective-permute-start.13 = (bf16[144,2048]{1,0:T(8,128)(2,1)S(1)}, bf16[144,2048]{1,0:T(8,128)(2,1)S(1)}, u32[]{:S(2)}, u32[]{:S(2)}) collective-permute-start(bf16[144,2048]{1,0:T(8,128)(2,1)S(1)} %shard_map.82.part), channel_id=1, source_target_pairs={{0,8},{1,9},{2,10},{3,11},{4,12},{5,13},{6,14},{7,15},{8,0},{9,1},... | collective-permute-start | bytes 1769480 | tf_op jit(solution)/shard_map/ppermute | solution.py:54
where the time goes:
time: 45.5 us; the launch traced here: 45.4 us
  waiting for transfers between devices  20.2 us (44%)
  starting transfers between devices  17.6 us (39%)
  Pallas kernels  5.87 us (13%)
  local copies, waits for them, and re-layouts  0.99 us (2%)
  between operations  0.73 us (2%)
    ppermute x14, waiting for transfers between devices, exchange(): return lax.ppermute(value, ('rep', 'shard'), pairs)  20.2 us
    ppermute x14, starting transfers between devices, exchange(): return lax.ppermute(value, ('rep', 'shard'), pairs)  17.6 us
    pallas_call x9, Pallas kernels, call(): pl.pallas_call(kernel, out_shape=outs, in_specs=[far if i in far_in else...  5.87 us
    unnamed x8, local copies, waits for them, and re-layouts  0.99 us
  transfers between devices with their start and end apart: 14, of which 11 were waited for; matrix products, arithmetic and copies ran while one was open for 0% of the time, Pallas kernels for 3%

commit v1 on v0

--- a/solution.py
+++ b/solution.py
@@ -58,24 +58,51 @@
     return exchange(value, lambda rep, shard: (rep ^ 1, shard))
 
 
-def across(value, dy, dx):
-    return exchange(value, lambda rep, shard: (rep ^ (2 * dx), shard ^ dy))
-
-
-def along_z(value, k):
-    return exchange(value, lambda rep, shard: (rep, shard ^ (2 * k)))
-
-
-SQUARE = ((1, 1), (0, 1), (1, 0))
-
-
-def far_first(levels):
-    return [k for k in range(levels - 1, 0, -1)]
+SQUARE = ((1, 1), (1, 0), (0, 1))
+LINE = (3, 2, 1)
+STEPS = tuple(zip(SQUARE, LINE))
+X_STEP = SQUARE.index((0, 1))
+STAY = ((0, 0), 0)
+
+
+def stage(value, step, square_core):
+    (dy, dx), k = step
+    return exchange(
+        value,
+        lambda rep, shard: (rep ^ (2 * dx), shard ^ dy) if rep & 1 == square_core else (rep, shard ^ (2 * k)),
+    )
+
+
+def wide_stage(value, step):
+    return stage(value, step, 0)
+
+
+def narrow_stage(value, step):
+    return stage(value, step, 1)
+
+
+def along_rest(value, k):
+    return exchange(value, lambda rep, shard: (rep, shard ^ (8 * k)))
 
 
 def place():
     rep, shard = lax.axis_index("rep"), lax.axis_index("shard")
-    return rep & 1, rep >> 1, shard & 1, shard >> 1
+    return rep & 1, rep >> 1, shard & 1, (shard >> 1) & 3, shard >> 3
+
+
+def in_half(step, group):
+    core, x, y, z, _ = place()
+    (dy, dx), k = step
+    first = core == 0
+    return (
+        jnp.where(first, y ^ dy, group >> 1), jnp.where(first, x ^ dx, group & 1), jnp.where(first, group, z ^ k),
+    )
+
+
+def group_of(step):
+    core, x, y, z, _ = place()
+    (dy, dx), k = step
+    return jnp.where(core == 0, z ^ k, 2 * (y ^ dy) + (x ^ dx))
 
 
 def block(index, size):
@@ -108,32 +135,44 @@
         out[:, at] = jnp.dot(turned[...], cots[:, at], preferred_element_type=F32)
 
 
-def square_kernel(kept, came, own, *pieces):
-    _, x, y, _ = place()
-    some_rows, quarter = own.shape
-    rows = kept.shape[0] // lax.axis_size("shard")
-    for (dy, dx), out in zip(((0, 0),) + SQUARE, (own,) + pieces):
-        cols = block(x ^ dx, quarter)
-        for z in range(some_rows // rows):
-            at = block(2 * z + (y ^ dy), rows)
-            out[z * rows:(z + 1) * rows, :] = (kept[at, cols] + came[at, cols].astype(F32)).astype(out.dtype)
-
-
-def line_kernel(steps, kept, *refs):
-    came, (own, *pieces) = refs[:len(SQUARE)], refs[len(SQUARE):]
-    z = place()[3]
-    rows = own.shape[0]
-    for k, out in zip([0] + steps, [own] + pieces):
-        at = block(z ^ k, rows)
+def wide_kernel(rows, kept, came, own, *pieces):
+    quarter = own.shape[1]
+    count = own.shape[0] // (4 * rows)
+    for step, out in zip((STAY,) + STEPS, (own,) + pieces):
+        for group in range(4):
+            y, x, z = in_half(step, group)
+            cols = block(x, quarter)
+            for w in range(count):
+                at = block(8 * w + 2 * z + y, rows)
+                total = kept[at, cols] + came[at, cols].astype(F32)
+                to = (group * count + w) * rows
+                out[to:to + rows, :] = total.astype(out.dtype)
+
+
+def narrow_kernel(kept, *refs):
+    came, (own, *pieces) = refs[:len(STEPS)], refs[len(STEPS):]
+    for step, out in zip((STAY,) + STEPS, [own] + pieces):
+        at = block(group_of(step), out.shape[0])
         total = kept[at, :]
         for ref in came:
             total += ref[at, :].astype(F32)
         out[...] = total.astype(out.dtype)
 
 
+def rest_kernel(kept, *refs):
+    came, outs = refs[:len(STEPS)], refs[len(STEPS):]
+    w = place()[4]
+    for k, out in enumerate(outs):
+        at = block(w ^ k, out.shape[0])
+        total = kept[at, :]
+        for ref in came:
+            total += ref[at, :].astype(F32)
+        out[...] = total.astype(out.dtype)
+
+
 def update_kernel(w, m, v, own, *refs):
     pieces, (new_w, grad) = refs[:-2], refs[-2:]
-    core, x, _, _ = place()
+    core, x, _, _, _ = place()
     total = own[...]
     for ref in pieces:
         total += ref[...].astype(F32)
@@ -143,28 +182,52 @@
     new_w[...] = adamw_weight(w[:, at], new_m, new_v)
 
 
-def pack_kernel(steps, grad, *refs):
+def rest_back_kernel(grad, *refs):
     pieces, (out, with_grad) = refs[:-2], refs[-2:]
-    z = place()[3]
-    rows, some_rows = grad.shape[0], out.shape[0]
-    for k, ref in zip([0] + steps, pieces):
-        at = block(z ^ k, rows)
+    w = place()[4]
+    rows, tail = grad.shape[0], out.shape[0]
+    for k, ref in enumerate(pieces):
+        at = block(w ^ k, rows)
         out[at, :] = ref[...]
         with_grad[at, :] = ref[...]
-    with_grad[some_rows:, :] = grad[...]
-
-
-def half_kernel(own, *refs):
+    with_grad[tail:, :] = grad[...]
+
+
+def narrow_back_kernel(own, *refs):
+    parts, (out, with_grad) = (own,) + refs[:-2], refs[-2:]
+    size = out.shape[0] // 4
+    for step, ref in zip((STAY,) + STEPS[::-1], parts):
+        at = block(group_of(step), size)
+        out[at, :] = ref[:size, :]
+        with_grad[at, :] = ref[:size, :]
+    with_grad[4 * size:, :] = own[size:, :]
+
+
+def wide_back_kernel(early, own, *refs):
     parts, out = (own,) + refs[:-1], refs[-1]
-    _, x, y, _ = place()
+    core, near, _, _, _ = place()
     rows = out.shape[0] // (lax.axis_size("shard") + 1)
-    some_rows, quarter = parts[-1].shape
-    for (dy, dx), ref in zip(((0, 0),) + SQUARE[::-1], parts):
-        cols = block(x ^ dx, quarter)
-        for z in range(some_rows // rows):
-            out[block(2 * z + (y ^ dy), rows), cols] = ref[z * rows:(z + 1) * rows, :]
-        if dy == 0:
-            out[2 * some_rows:, cols] = ref[some_rows:, :]
+    all_rows, quarter = out.shape[0] - rows, own.shape[1]
+    size = all_rows // 2
+    count = size // (4 * rows)
+    for step, ref in zip((STAY,) + STEPS[::-1], parts):
+        for group in range(4):
+            y, x, z = in_half(step, group)
+            for w in range(count):
+                at = (group * count + w) * rows
+                out[block(8 * w + 2 * z + y, rows), block(x, quarter)] = ref[at:at + rows, :]
+    out[all_rows:, block(near, quarter)] = own[size:, :]
+    late = parts[len(STEPS) - X_STEP]
+    far = block(1 - near, quarter)
+    narrow = early.shape[0] - rows
+
+    @pl.when(core == 0)
+    def _():
+        out[all_rows:, far] = late[size:, :]
+
+    @pl.when(core != 0)
+    def _():
+        out[all_rows:, far] = early[narrow:, :]
 
 
 def write_kernel(away, part, m, v, *refs):
@@ -185,10 +248,10 @@
 def body(hidden_acts, out_cotangent, weight, first_moment, second_moment):
     rows, width = weight.shape
     tokens, all_rows = hidden_acts.shape
-    some_rows, levels = all_rows // 2, lax.axis_size("shard") // 2
     half, quarter = width // 2, width // 4
     count = half // CHUNK
-    steps = far_first(levels)
+    rest = lax.axis_size("shard") // 8
+    wide_rows, narrow_rows = all_rows // 2, all_rows // 8
 
     away, turned, cots = call(
         load_kernel,
@@ -204,29 +267,34 @@
     came = to_sibling(away)
     kept = call(product_kernel, [shape((all_rows, half), F32)], turned, cots)[0]
 
-    own, *pieces = call(
-        square_kernel,
-        [shape((some_rows, quarter), F32)] + [shape((some_rows, quarter), BF16)] * len(SQUARE), kept, came,
-    )
-    came = [across(piece, *step) for step, piece in zip(SQUARE, pieces)]
-    own, *pieces = call(
-        functools.partial(line_kernel, steps),
-        [shape((rows, quarter), F32)] + [shape((rows, quarter), BF16)] * (levels - 1), own, *came,
-    )
-    pieces = [along_z(piece, k) for k, piece in zip(steps, pieces)]
+    def split(kernel, size, parts, *args):
+        kept, sent = shape((size, quarter), F32), shape((size, quarter), BF16)
+        return call(kernel, [kept] + [sent] * (parts - 1), *args)
+
+    own, *pieces = split(functools.partial(wide_kernel, rows), wide_rows, 4, kept, came)
+    came = [wide_stage(piece, step) for step, piece in zip(STEPS, pieces)]
+    own, *pieces = split(narrow_kernel, narrow_rows, 4, own, *came)
+    came = [narrow_stage(piece, step) for step, piece in zip(STEPS, pieces)]
+    if rest > 1:
+        own, *pieces = split(rest_kernel, rows, rest, own, *came)
+        came = [along_rest(piece, k + 1) for k, piece in enumerate(pieces)]
     new_w, grad = call(
-        update_kernel, [shape((rows, quarter), BF16)] * 2,
-        weight, first_moment, second_moment, own, *pieces,
-    )
-
-    back = steps[::-1]
-    pieces = [new_w] + [along_z(new_w, k) for k in back]
-    mine, with_grad = call(
-        functools.partial(pack_kernel, back),
-        [shape((some_rows, quarter), BF16), shape((some_rows + rows, quarter), BF16)], grad, *pieces,
-    )
-    parts = [across(mine if dy else with_grad, dy, dx) for dy, dx in SQUARE[::-1]]
-    part = call(half_kernel, [shape((all_rows + rows, half), BF16)], with_grad, *parts)[0]
+        update_kernel, [shape((rows, quarter), BF16)] * 2, weight, first_moment, second_moment, own, *came,
+    )
+
+    def gathered(kernel, size, *args):
+        return call(kernel, [shape((size, quarter), BF16), shape((size + rows, quarter), BF16)], *args)
+
+    def back(send, part, with_grad):
+        return [send(with_grad if i == X_STEP else part, STEPS[i]) for i in reversed(range(len(STEPS)))]
+
+    pieces = [along_rest(new_w, k) for k in range(1, rest)]
+    part, with_grad = gathered(rest_back_kernel, narrow_rows, grad, new_w, *pieces)
+    came = back(narrow_stage, part, with_grad)
+    early = came[len(STEPS) - 1 - X_STEP]
+    part, with_grad = gathered(narrow_back_kernel, wide_rows, with_grad, *came)
+    came = back(wide_stage, part, with_grad)
+    part = call(wide_back_kernel, [shape((all_rows + rows, half), BF16)], early, with_grad, *came)[0]
     other = to_sibling(part)
     results = [shape((all_rows, width), BF16), shape((rows, width), F32), shape((rows, width), F32)]
     scratch = [pltpu.VMEM((rows, half), F32), pltpu.VMEM((rows, half), F32), pltpu.SemaphoreType.DMA((3,))]

time: 45.5 us -> 48.9 us (1.075)
  waiting for transfers between devices: 20.2 us -> 22.1 us
  starting transfers between devices: 17.6 us -> 19.1 us
    ppermute x14, waiting for transfers between devices: 20.2 us -> 22.1 us  [exchange(): return lax.ppermute(value, ('rep', 'shard'), pairs)]
    ppermute x14, starting transfers between devices: 17.6 us -> 19.1 us  [exchange(): return lax.ppermute(value, ('rep', 'shard'), pairs)]
    pallas_call x9 -> x10, Pallas kernels: 5.87 us -> 5.89 us  [call(): pl.pallas_call(kernel, out_shape=outs, in_specs=[far if i in far_in else...]
where the time goes in v1:
time: 48.9 us; the launch traced here: 48.8 us
  waiting for transfers between devices  22.1 us (45%)
  starting transfers between devices  19.1 us (39%)
  Pallas kernels  5.89 us (12%)
  local copies, waits for them, and re-layouts  0.99 us (2%)
  between operations  0.75 us (2%)
    ppermute x14, waiting for transfers between devices, exchange(): return lax.ppermute(value, ('rep', 'shard'), pairs)  22.1 us
    ppermute x14, starting transfers between devices, exchange(): return lax.ppermute(value, ('rep', 'shard'), pairs)  19.1 us
    pallas_call x10, Pallas kernels, call(): pl.pallas_call(kernel, out_shape=outs, in_specs=[far if i in far_in else...  5.89 us
    unnamed x8, local copies, waits for them, and re-layouts  0.99 us
  transfers between devices with their start and end apart: 14, of which 11 were waited for; matrix products, arithmetic and copies ran while one was open for 0% of the time, Pallas kernels for 3%

profile of v1, /device:TPU:0, one launch (start us, length us, event | category | flops | bytes accessed | tf_op | source)
XLA Modules:
  0.0 48.8 jit_solution(7024060282013789848)
XLA Ops:
  0.7 1.0 %copy-done.2 = bf16[768,128]{1,0:T(8,128)(2,1)S(1)} copy-done((bf16[768,128]{1,0:T(8,128)(2,1)S(1)}, bf16[768,128]{1,0:T(8,128)(2,1)}, u32[]{:S(2)}) %copy-start.2) | copy-done | bytes 196632
  1.6 3.2 %shard_map.76 = (bf16[128,2048]{1,0:T(8,128)(2,1)S(1)}, bf16[128,768]{1,0:T(8,128)(2,1)S(1)}, bf16[768,2048]{1,0:T(8,128)(2,1)S(1)}) custom-call(bf16[768,128]{1,0:T(8,128)(2,1)S(1)} %copy-done.2, bf16[768,4096]{1,0:T(8,128)(2,1)} %cots_ref.1), custom_call_target="tpu_custom_call" | custom-call | tf_op jit(solution)/shard_map/pallas_call | solution.py:36
  4.8 0.5 %collective-permute-start = (bf16[128,2048]{1,0:T(8,128)(2,1)S(1)}, bf16[128,2048]{1,0:T(8,128)(2,1)S(1)}, u32[]{:S(2)}, u32[]{:S(2)}) collective-permute-start(bf16[128,2048]{1,0:T(8,128)(2,1)S(1)} %get-tuple-element.25), channel_id=1, source_target_pairs={{0,8},{1,9},{2,10},{3,11},{4,12},{5,13},{6,14},{7,15},{8,0},{9,1},... | collective-permute-start | bytes 1572872 | tf_op jit(solution)/shard_map/ppermute | solution.py:54
  5.3 0.6 %shard_map.77.kept = f32[128,2048]{1,0:T(8,128)S(1)} custom-call(bf16[128,768]{1,0:T(8,128)(2,1)S(1)} %get-tuple-element.23.turned, bf16[768,2048]{1,0:T(8,128)(2,1)S(1)} %get-tuple-element.24.cots), custom_call_target="tpu_custom_call" | custom-call | tf_op jit(solution)/shard_map/pallas_call | solution.py:36
  5.9 1.0 %collective-permute-done.came = bf16[128,2048]{1,0:T(8,128)(2,1)S(1)} collective-permute-done((bf16[128,2048]{1,0:T(8,128)(2,1)S(1)}, bf16[128,2048]{1,0:T(8,128)(2,1)S(1)}, u32[]{:S(2)}, u32[]{:S(2)}) %collective-permute-start) | collective-permute-done | bytes 524320 | tf_op jit(solution)/shard_map/ppermute | solution.py:54
  7.0 3.9 %collective-permute-start.1 = (bf16[64,1024]{1,0:T(8,128)(2,1)S(1)}, bf16[64,1024]{1,0:T(8,128)(2,1)S(1)}, u32[]{:S(2)}, u32[]{:S(2)}) collective-permute-start(bf16[64,1024]{1,0:T(8,128)(2,1)S(1)} %get-tuple-element.27), channel_id=1, source_target_pairs={{0,17},{1,16},{2,19},{3,18},{4,21},{5,20},{6,23},{7,22},{8,14},{9,... | collective-permute-start | bytes 393224 | tf_op jit(solution)/shard_map/ppermute | solution.py:54
  10.8 0.5 %collective-permute-start.2 = (bf16[64,1024]{1,0:T(8,128)(2,1)S(1)}, bf16[64,1024]{1,0:T(8,128)(2,1)S(1)}, u32[]{:S(2)}, u32[]{:S(2)}) collective-permute-start(bf16[64,1024]{1,0:T(8,128)(2,1)S(1)} %get-tuple-element.28), channel_id=1, source_target_pairs={{0,1},{1,0},{2,3},{3,2},{4,5},{5,4},{6,7},{7,6},{8,12},{9,13},{10,... | collective-permute-start | bytes 393224 | tf_op jit(solution)/shard_map/ppermute | solution.py:54
  11.5 2.3 %collective-permute-done.1.refs_0_ = bf16[64,1024]{1,0:T(8,128)(2,1)S(1)} collective-permute-done((bf16[64,1024]{1,0:T(8,128)(2,1)S(1)}, bf16[64,1024]{1,0:T(8,128)(2,1)S(1)}, u32[]{:S(2)}, u32[]{:S(2)}) %collective-permute-start.1) | collective-permute-done | bytes 131104 | tf_op jit(solution)/shard_map/ppermute | solution.py:54
  13.8 2.0 %collective-permute-done.2.refs_1_ = bf16[64,1024]{1,0:T(8,128)(2,1)S(1)} collective-permute-done((bf16[64,1024]{1,0:T(8,128)(2,1)S(1)}, bf16[64,1024]{1,0:T(8,128)(2,1)S(1)}, u32[]{:S(2)}, u32[]{:S(2)}) %collective-permute-start.2) | collective-permute-done | bytes 131104 | tf_op jit(solution)/shard_map/ppermute | solution.py:54
  15.8 0.5 %collective-permute-done.3.refs_2_ = bf16[64,1024]{1,0:T(8,128)(2,1)S(1)} collective-permute-done((bf16[64,1024]{1,0:T(8,128)(2,1)S(1)}, bf16[64,1024]{1,0:T(8,128)(2,1)S(1)}, u32[]{:S(2)}, u32[]{:S(2)}) %collective-permute-start.3) | collective-permute-done | bytes 131104 | tf_op jit(solution)/shard_map/ppermute | solution.py:54
  16.4 3.7 %collective-permute-start.4 = (bf16[16,1024]{1,0:T(8,128)(2,1)S(1)}, bf16[16,1024]{1,0:T(8,128)(2,1)S(1)}, u32[]{:S(2)}, u32[]{:S(2)}) collective-permute-start(bf16[16,1024]{1,0:T(8,128)(2,1)S(1)} %get-tuple-element.31), channel_id=1, source_target_pairs={{0,6},{1,7},{2,4},{3,5},{4,2},{5,3},{6,0},{7,1},{8,25},{9,24},{10,... | collective-permute-start | bytes 98312 | tf_op jit(solution)/shard_map/ppermute | solution.py:54
  20.0 0.8 %collective-permute-start.6 = (bf16[16,1024]{1,0:T(8,128)(2,1)S(1)}, bf16[16,1024]{1,0:T(8,128)(2,1)S(1)}, u32[]{:S(2)}, u32[]{:S(2)}) collective-permute-start(bf16[16,1024]{1,0:T(8,128)(2,1)S(1)} %get-tuple-element.33), channel_id=1, source_target_pairs={{0,2},{1,3},{2,0},{3,1},{4,6},{5,7},{6,4},{7,5},{8,24},{9,25},{10,... | collective-permute-start | bytes 98312 | tf_op jit(solution)/shard_map/ppermute | solution.py:54
  20.8 1.3 %collective-permute-done.4.refs_0_ = bf16[16,1024]{1,0:T(8,128)(2,1)S(1)} collective-permute-done((bf16[16,1024]{1,0:T(8,128)(2,1)S(1)}, bf16[16,1024]{1,0:T(8,128)(2,1)S(1)}, u32[]{:S(2)}, u32[]{:S(2)}) %collective-permute-start.4) | collective-permute-done | bytes 32800 | tf_op jit(solution)/shard_map/ppermute | solution.py:54
  22.2 2.7 %collective-permute-done.5.refs_1_ = bf16[16,1024]{1,0:T(8,128)(2,1)S(1)} collective-permute-done((bf16[16,1024]{1,0:T(8,128)(2,1)S(1)}, bf16[16,1024]{1,0:T(8,128)(2,1)S(1)}, u32[]{:S(2)}, u32[]{:S(2)}) %collective-permute-start.5) | collective-permute-done | bytes 32800 | tf_op jit(solution)/shard_map/ppermute | solution.py:54
  25.1 3.5 %collective-permute-start.9 = (bf16[16,1024]{1,0:T(8,128)(2,1)S(1)}, bf16[16,1024]{1,0:T(8,128)(2,1)S(1)}, u32[]{:S(2)}, u32[]{:S(2)}) collective-permute-start(bf16[16,1024]{1,0:T(8,128)(2,1)S(1)} %get-tuple-element.37), channel_id=1, source_target_pairs={{0,6},{1,7},{2,4},{3,5},{4,2},{5,3},{6,0},{7,1},{8,25},{9,24},{10,... | collective-permute-start | bytes 98312 | tf_op jit(solution)/shard_map/ppermute | solution.py:54
  28.5 2.6 %collective-permute-done.9.refs_2_ = bf16[16,1024]{1,0:T(8,128)(2,1)S(1)} collective-permute-done((bf16[16,1024]{1,0:T(8,128)(2,1)S(1)}, bf16[16,1024]{1,0:T(8,128)(2,1)S(1)}, u32[]{:S(2)}, u32[]{:S(2)}) %collective-permute-start.9) | collective-permute-done | bytes 32800 | tf_op jit(solution)/shard_map/ppermute | solution.py:54
  31.1 2.5 %collective-permute-done.8.refs_1_ = bf16[16,1024]{1,0:T(8,128)(2,1)S(1)} collective-permute-done((bf16[16,1024]{1,0:T(8,128)(2,1)S(1)}, bf16[16,1024]{1,0:T(8,128)(2,1)S(1)}, u32[]{:S(2)}, u32[]{:S(2)}) %collective-permute-start.8) | collective-permute-done | bytes 32800 | tf_op jit(solution)/shard_map/ppermute | solution.py:54
  33.7 1.0 %collective-permute-start.10 = (bf16[80,1024]{1,0:T(8,128)(2,1)S(1)}, bf16[80,1024]{1,0:T(8,128)(2,1)S(1)}, u32[]{:S(2)}, u32[]{:S(2)}) collective-permute-start(bf16[80,1024]{1,0:T(8,128)(2,1)S(1)} %get-tuple-element.38.own), channel_id=1, source_target_pairs={{0,16},{1,17},{2,18},{3,19},{4,20},{5,21},{6,22},{7,23},{8,10},{9,... | collective-permute-start | bytes 491528 | tf_op jit(solution)/shard_map/ppermute | solution.py:54
  34.7 4.9 %collective-permute-start.12 = (bf16[64,1024]{1,0:T(8,128)(2,1)S(1)}, bf16[64,1024]{1,0:T(8,128)(2,1)S(1)}, u32[]{:S(2)}, u32[]{:S(2)}) collective-permute-start(bf16[64,1024]{1,0:T(8,128)(2,1)S(1)} %get-tuple-element.39), channel_id=1, source_target_pairs={{0,17},{1,16},{2,19},{3,18},{4,21},{5,20},{6,23},{7,22},{8,14},{9,... | collective-permute-start | bytes 393224 | tf_op jit(solution)/shard_map/ppermute | solution.py:54
  39.6 4.8 %collective-permute-done.12.refs_2_ = bf16[64,1024]{1,0:T(8,128)(2,1)S(1)} collective-permute-done((bf16[64,1024]{1,0:T(8,128)(2,1)S(1)}, bf16[64,1024]{1,0:T(8,128)(2,1)S(1)}, u32[]{:S(2)}, u32[]{:S(2)}) %collective-permute-start.12) | collective-permute-done | bytes 131104 | tf_op jit(solution)/shard_map/ppermute | solution.py:54
  44.4 1.3 %collective-permute-done.11.refs_1_ = bf16[64,1024]{1,0:T(8,128)(2,1)S(1)} collective-permute-done((bf16[64,1024]{1,0:T(8,128)(2,1)S(1)}, bf16[64,1024]{1,0:T(8,128)(2,1)S(1)}, u32[]{:S(2)}, u32[]{:S(2)}) %collective-permute-start.11) | collective-permute-done | bytes 131104 | tf_op jit(solution)/shard_map/ppermute | solution.py:54
  45.9 0.9 %shard_map.84 = (bf16[128,4096]{1,0:T(8,128)(2,1)}, f32[16,4096]{1,0:T(8,128)}, f32[16,4096]{1,0:T(8,128)}) custom-call(bf16[144,2048]{1,0:T(8,128)(2,1)S(1)} %shard_map.83.part, f32[16,4096]{1,0:T(8,128)S(1)} %copy-done, f32[16,4096]{1,0:T(8,128)S(1)} %copy-done.1), custom_call_target="tpu_custom_call" | custom-call | tf_op jit(solution)/shard_map/pallas_call | solution.py:36
  46.8 1.1 %collective-permute-done.13.part = bf16[144,2048]{1,0:T(8,128)(2,1)S(1)} collective-permute-done((bf16[144,2048]{1,0:T(8,128)(2,1)S(1)}, bf16[144,2048]{1,0:T(8,128)(2,1)S(1)}, u32[]{:S(2)}, u32[]{:S(2)}) %collective-permute-start.13) | collective-permute-done | bytes 589856 | tf_op jit(solution)/shard_map/ppermute | solution.py:54
  47.9 0.9 %shard_map.85 = (bf16[128,4096]{1,0:T(8,128)(2,1)}, f32[16,4096]{1,0:T(8,128)}, f32[16,4096]{1,0:T(8,128)}) custom-call(bf16[144,2048]{1,0:T(8,128)(2,1)S(1)} %collective-permute-done.13.part, f32[16,4096]{1,0:T(8,128)S(1)} %copy-done, f32[16,4096]{1,0:T(8,128)S(1)} %copy-done.1, ...), custom_call_target="tpu_custom_call", output_to_operand_aliasing={{0}: (3, {}), {1}: (4, {}), {2}: (5, {})} | custom-call | tf_op jit(solution)/shard_map/pallas_call | solution.py:36
  (22 shorter events, 0.6 us)
Async XLA Ops:
  0.6 24.2 %copy-start.1 = (f32[16,4096]{1,0:T(8,128)S(1)}, f32[16,4096]{1,0:T(8,128)}, u32[]{:S(2)}) copy-start(f32[16,4096]{1,0:T(8,128)} %v.5) | copy-start | bytes 786436
  0.6 24.2 %copy-start = (f32[16,4096]{1,0:T(8,128)S(1)}, f32[16,4096]{1,0:T(8,128)}, u32[]{:S(2)}) copy-start(f32[16,4096]{1,0:T(8,128)} %m.5) | copy-start | bytes 786436
  0.7 1.0 %copy-start.2 = (bf16[768,128]{1,0:T(8,128)(2,1)S(1)}, bf16[768,128]{1,0:T(8,128)(2,1)}, u32[]{:S(2)}) copy-start(bf16[768,128]{1,0:T(8,128)(2,1)} %acts_ref.1) | copy-start | bytes 589828
  1.6 23.2 %copy-start.3 = (bf16[16,4096]{1,0:T(8,128)(2,1)S(1)}, bf16[16,4096]{1,0:T(8,128)(2,1)}, u32[]{:S(2)}) copy-start(bf16[16,4096]{1,0:T(8,128)(2,1)} %w.1) | copy-start | bytes 393220
  4.8 2.1 %collective-permute-start = (bf16[128,2048]{1,0:T(8,128)(2,1)S(1)}, bf16[128,2048]{1,0:T(8,128)(2,1)S(1)}, u32[]{:S(2)}, u32[]{:S(2)}) collective-permute-start(bf16[128,2048]{1,0:T(8,128)(2,1)S(1)} %get-tuple-element.25), channel_id=1, source_target_pairs={{0,8},{1,9},{2,10},{3,11},{4,12},{5,13},{6,14},{7,15},{8,0},{9,1},... | collective-permute-start | bytes 1572872 | tf_op jit(solution)/shard_map/ppermute | solution.py:54
  7.0 6.8 %collective-permute-start.1 = (bf16[64,1024]{1,0:T(8,128)(2,1)S(1)}, bf16[64,1024]{1,0:T(8,128)(2,1)S(1)}, u32[]{:S(2)}, u32[]{:S(2)}) collective-permute-start(bf16[64,1024]{1,0:T(8,128)(2,1)S(1)} %get-tuple-element.27), channel_id=1, source_target_pairs={{0,17},{1,16},{2,19},{3,18},{4,21},{5,20},{6,23},{7,22},{8,14},{9,... | collective-permute-start | bytes 393224 | tf_op jit(solution)/shard_map/ppermute | solution.py:54
  10.8 5.0 %collective-permute-start.2 = (bf16[64,1024]{1,0:T(8,128)(2,1)S(1)}, bf16[64,1024]{1,0:T(8,128)(2,1)S(1)}, u32[]{:S(2)}, u32[]{:S(2)}) collective-permute-start(bf16[64,1024]{1,0:T(8,128)(2,1)S(1)} %get-tuple-element.28), channel_id=1, source_target_pairs={{0,1},{1,0},{2,3},{3,2},{4,5},{5,4},{6,7},{7,6},{8,12},{9,13},{10,... | collective-permute-start | bytes 393224 | tf_op jit(solution)/shard_map/ppermute | solution.py:54
  11.3 5.0 %collective-permute-start.3 = (bf16[64,1024]{1,0:T(8,128)(2,1)S(1)}, bf16[64,1024]{1,0:T(8,128)(2,1)S(1)}, u32[]{:S(2)}, u32[]{:S(2)}) collective-permute-start(bf16[64,1024]{1,0:T(8,128)(2,1)S(1)} %get-tuple-element.29), channel_id=1, source_target_pairs={{0,16},{1,17},{2,18},{3,19},{4,20},{5,21},{6,22},{7,23},{8,10},{9,... | collective-permute-start | bytes 393224 | tf_op jit(solution)/shard_map/ppermute | solution.py:54
  16.4 5.8 %collective-permute-start.4 = (bf16[16,1024]{1,0:T(8,128)(2,1)S(1)}, bf16[16,1024]{1,0:T(8,128)(2,1)S(1)}, u32[]{:S(2)}, u32[]{:S(2)}) collective-permute-start(bf16[16,1024]{1,0:T(8,128)(2,1)S(1)} %get-tuple-element.31), channel_id=1, source_target_pairs={{0,6},{1,7},{2,4},{3,5},{4,2},{5,3},{6,0},{7,1},{8,25},{9,24},{10,... | collective-permute-start | bytes 98312 | tf_op jit(solution)/shard_map/ppermute | solution.py:54
  20.0 4.8 %collective-permute-start.5 = (bf16[16,1024]{1,0:T(8,128)(2,1)S(1)}, bf16[16,1024]{1,0:T(8,128)(2,1)S(1)}, u32[]{:S(2)}, u32[]{:S(2)}) collective-permute-start(bf16[16,1024]{1,0:T(8,128)(2,1)S(1)} %get-tuple-element.32), channel_id=1, source_target_pairs={{0,4},{1,5},{2,6},{3,7},{4,0},{5,1},{6,2},{7,3},{8,9},{9,8},{10,11... | collective-permute-start | bytes 98312 | tf_op jit(solution)/shard_map/ppermute | solution.py:54
  20.0 4.8 %collective-permute-start.6 = (bf16[16,1024]{1,0:T(8,128)(2,1)S(1)}, bf16[16,1024]{1,0:T(8,128)(2,1)S(1)}, u32[]{:S(2)}, u32[]{:S(2)}) collective-permute-start(bf16[16,1024]{1,0:T(8,128)(2,1)S(1)} %get-tuple-element.33), channel_id=1, source_target_pairs={{0,2},{1,3},{2,0},{3,1},{4,6},{5,7},{6,4},{7,5},{8,24},{9,25},{10,... | collective-permute-start | bytes 98312 | tf_op jit(solution)/shard_map/ppermute | solution.py:54
  25.0 8.7 %collective-permute-start.7 = (bf16[32,1024]{1,0:T(8,128)(2,1)S(1)}, bf16[32,1024]{1,0:T(8,128)(2,1)S(1)}, u32[]{:S(2)}, u32[]{:S(2)}) collective-permute-start(bf16[32,1024]{1,0:T(8,128)(2,1)S(1)} %get-tuple-element.36.own), channel_id=1, source_target_pairs={{0,2},{1,3},{2,0},{3,1},{4,6},{5,7},{6,4},{7,5},{8,24},{9,25},{10,... | collective-permute-start | bytes 196616 | tf_op jit(solution)/shard_map/ppermute | solution.py:54
  25.1 6.1 %collective-permute-start.9 = (bf16[16,1024]{1,0:T(8,128)(2,1)S(1)}, bf16[16,1024]{1,0:T(8,128)(2,1)S(1)}, u32[]{:S(2)}, u32[]{:S(2)}) collective-permute-start(bf16[16,1024]{1,0:T(8,128)(2,1)S(1)} %get-tuple-element.37), channel_id=1, source_target_pairs={{0,6},{1,7},{2,4},{3,5},{4,2},{5,3},{6,0},{7,1},{8,25},{9,24},{10,... | collective-permute-start | bytes 98312 | tf_op jit(solution)/shard_map/ppermute | solution.py:54
  28.5 5.1 %collective-permute-start.8 = (bf16[16,1024]{1,0:T(8,128)(2,1)S(1)}, bf16[16,1024]{1,0:T(8,128)(2,1)S(1)}, u32[]{:S(2)}, u32[]{:S(2)}) collective-permute-start(bf16[16,1024]{1,0:T(8,128)(2,1)S(1)} %get-tuple-element.37), channel_id=1, source_target_pairs={{0,4},{1,5},{2,6},{3,7},{4,0},{5,1},{6,2},{7,3},{8,9},{9,8},{10,11... | collective-permute-start | bytes 98312 | tf_op jit(solution)/shard_map/ppermute | solution.py:54
  33.7 12.0 %collective-permute-start.10 = (bf16[80,1024]{1,0:T(8,128)(2,1)S(1)}, bf16[80,1024]{1,0:T(8,128)(2,1)S(1)}, u32[]{:S(2)}, u32[]{:S(2)}) collective-permute-start(bf16[80,1024]{1,0:T(8,128)(2,1)S(1)} %get-tuple-element.38.own), channel_id=1, source_target_pairs={{0,16},{1,17},{2,18},{3,19},{4,20},{5,21},{6,22},{7,23},{8,10},{9,... | collective-permute-start | bytes 491528 | tf_op jit(solution)/shard_map/ppermute | solution.py:54
  34.7 9.7 %collective-permute-start.12 = (bf16[64,1024]{1,0:T(8,128)(2,1)S(1)}, bf16[64,1024]{1,0:T(8,128)(2,1)S(1)}, u32[]{:S(2)}, u32[]{:S(2)}) collective-permute-start(bf16[64,1024]{1,0:T(8,128)(2,1)S(1)} %get-tuple-element.39), channel_id=1, source_target_pairs={{0,17},{1,16},{2,19},{3,18},{4,21},{5,20},{6,23},{7,22},{8,14},{9,... | collective-permute-start | bytes 393224 | tf_op jit(solution)/shard_map/ppermute | solution.py:54
  39.6 6.1 %collective-permute-start.11 = (bf16[64,1024]{1,0:T(8,128)(2,1)S(1)}, bf16[64,1024]{1,0:T(8,128)(2,1)S(1)}, u32[]{:S(2)}, u32[]{:S(2)}) collective-permute-start(bf16[64,1024]{1,0:T(8,128)(2,1)S(1)} %get-tuple-element.39), channel_id=1, source_target_pairs={{0,1},{1,0},{2,3},{3,2},{4,5},{5,4},{6,7},{7,6},{8,12},{9,13},{10,... | collective-permute-start | bytes 393224 | tf_op jit(solution)/shard_map/ppermute | solution.py:54
  45.8 2.1 %collective-permute-start.13 = (bf16[144,2048]{1,0:T(8,128)(2,1)S(1)}, bf16[144,2048]{1,0:T(8,128)(2,1)S(1)}, u32[]{:S(2)}, u32[]{:S(2)}) collective-permute-start(bf16[144,2048]{1,0:T(8,128)(2,1)S(1)} %shard_map.83.part), channel_id=1, source_target_pairs={{0,8},{1,9},{2,10},{3,11},{4,12},{5,13},{6,14},{7,15},{8,0},{9,1},... | collective-permute-start | bytes 1769480 | tf_op jit(solution)/shard_map/ppermute | solution.py:54

commit v2 on v1

--- a/solution.py
+++ b/solution.py
@@ -10,7 +10,7 @@
 F32 = jnp.float32
 BF16 = jnp.bfloat16
 CHUNK = 512
-LOAD_LIMIT = 48 * 1024 * 1024
+LOAD_LIMIT = 45 * 1024 * 1024
 
 
 def adamw_moments(first_moment, second_moment, grad):
@@ -109,24 +109,22 @@
     return pl.ds(pl.multiple_of(index * size, size), size)
 
 
-def load_kernel(acts_ref, cots_ref, out, turned, kept_cots, acts, cots, sems):
+def load_kernel(cots_ref, away, kept, sems):
     core = place()[0]
-    count = cots.shape[0]
-    copies = [pltpu.make_async_copy(acts_ref, acts, sems.at[count])]
-    for i in range(count):
-        source = cots_ref.at[:, block((1 - core) * count + i, CHUNK)]
-        copies.append(pltpu.make_async_copy(source, cots.at[i], sems.at[i]))
-    own = cots_ref.at[:, block(core, kept_cots.shape[1])]
-    copies.append(pltpu.make_async_copy(own, kept_cots, sems.at[count + 1]))
+    copies = []
+    for out, side in ((away, 1 - core), (kept, core)):
+        source = cots_ref.at[:, block(side, out.shape[1])]
+        copies.append(pltpu.make_async_copy(source, out, sems.at[len(copies)]))
+        copies[-1].start()
     for copy in copies:
-        copy.start()
-    copies[0].wait()
+        copy.wait()
+
+
+def away_kernel(acts, cots, out, turned):
     turned[...] = acts[...].T
-    for i in range(count):
-        copies[i + 1].wait()
-        term = jnp.dot(turned[...], cots[i], preferred_element_type=F32)
-        out[:, i * CHUNK:(i + 1) * CHUNK] = term.astype(out.dtype)
-    copies[-1].wait()
+    for i in range(out.shape[1] // CHUNK):
+        at = slice(i * CHUNK, (i + 1) * CHUNK)
+        out[:, at] = jnp.dot(turned[...], cots[:, at], preferred_element_type=F32).astype(BF16)
 
 
 def product_kernel(turned, cots, out):
@@ -182,25 +180,26 @@
     new_w[...] = adamw_weight(w[:, at], new_m, new_v)
 
 
+def put(outs, at, value):
+    for out in outs:
+        out[at, :] = value
+
+
 def rest_back_kernel(grad, *refs):
-    pieces, (out, with_grad) = refs[:-2], refs[-2:]
+    pieces, outs = refs[:-len(STEPS)], refs[-len(STEPS):]
     w = place()[4]
-    rows, tail = grad.shape[0], out.shape[0]
+    rows, tail = grad.shape[0], outs[0].shape[0]
     for k, ref in enumerate(pieces):
-        at = block(w ^ k, rows)
-        out[at, :] = ref[...]
-        with_grad[at, :] = ref[...]
-    with_grad[tail:, :] = grad[...]
-
-
-def narrow_back_kernel(own, *refs):
-    parts, (out, with_grad) = (own,) + refs[:-2], refs[-2:]
-    size = out.shape[0] // 4
-    for step, ref in zip((STAY,) + STEPS[::-1], parts):
-        at = block(group_of(step), size)
-        out[at, :] = ref[:size, :]
-        with_grad[at, :] = ref[:size, :]
-    with_grad[4 * size:, :] = own[size:, :]
+        put(outs, block(w ^ k, rows), ref[...])
+    outs[X_STEP][tail:, :] = grad[...]
+
+
+def narrow_back_kernel(_, own, *refs):
+    parts, outs = (own,) + refs[:-len(STEPS)], refs[-len(STEPS):]
+    size = outs[0].shape[0] // 4
+    for step, ref in zip((STAY,) + STEPS, parts):
+        put(outs, block(group_of(step), size), ref[:size, :])
+    outs[X_STEP][4 * size:, :] = own[size:, :]
 
 
 def wide_back_kernel(early, own, *refs):
@@ -210,14 +209,14 @@
     all_rows, quarter = out.shape[0] - rows, own.shape[1]
     size = all_rows // 2
     count = size // (4 * rows)
-    for step, ref in zip((STAY,) + STEPS[::-1], parts):
+    for step, ref in zip((STAY,) + STEPS, parts):
         for group in range(4):
             y, x, z = in_half(step, group)
             for w in range(count):
                 at = (group * count + w) * rows
                 out[block(8 * w + 2 * z + y, rows), block(x, quarter)] = ref[at:at + rows, :]
     out[all_rows:, block(near, quarter)] = own[size:, :]
-    late = parts[len(STEPS) - X_STEP]
+    late = parts[1 + X_STEP]
     far = block(1 - near, quarter)
     narrow = early.shape[0] - rows
 
@@ -249,20 +248,15 @@
     rows, width = weight.shape
     tokens, all_rows = hidden_acts.shape
     half, quarter = width // 2, width // 4
-    count = half // CHUNK
     rest = lax.axis_size("shard") // 8
     wide_rows, narrow_rows = all_rows // 2, all_rows // 8
 
-    away, turned, cots = call(
-        load_kernel,
-        [shape((all_rows, half), BF16), shape((all_rows, tokens), BF16), shape((tokens, half), BF16)],
-        hidden_acts, out_cotangent, far_in=(0, 1),
-        scratch=[
-            pltpu.VMEM((tokens, all_rows), BF16),
-            pltpu.VMEM((count, tokens, CHUNK), BF16),
-            pltpu.SemaphoreType.DMA((count + 2,)),
-        ],
-        limit=LOAD_LIMIT,
+    loaded = [shape((tokens, half), BF16)] * 2
+    away_cots, cots = call(
+        load_kernel, loaded, out_cotangent, far_in=(0,), scratch=[pltpu.SemaphoreType.DMA((2,))], limit=LOAD_LIMIT,
+    )
+    away, turned = call(
+        away_kernel, [shape((all_rows, half), BF16), shape((all_rows, tokens), BF16)], hidden_acts, away_cots,
     )
     came = to_sibling(away)
     kept = call(product_kernel, [shape((all_rows, half), F32)], turned, cots)[0]
@@ -283,18 +277,18 @@
     )
 
     def gathered(kernel, size, *args):
-        return call(kernel, [shape((size, quarter), BF16), shape((size + rows, quarter), BF16)], *args)
-
-    def back(send, part, with_grad):
-        return [send(with_grad if i == X_STEP else part, STEPS[i]) for i in reversed(range(len(STEPS)))]
-
+        sizes = [size + rows if i == X_STEP else size for i in range(len(STEPS))]
+        return call(kernel, [shape((size, quarter), BF16) for size in sizes], *args)
+
+    level = to_sibling(grad)
     pieces = [along_rest(new_w, k) for k in range(1, rest)]
-    part, with_grad = gathered(rest_back_kernel, narrow_rows, grad, new_w, *pieces)
-    came = back(narrow_stage, part, with_grad)
-    early = came[len(STEPS) - 1 - X_STEP]
-    part, with_grad = gathered(narrow_back_kernel, wide_rows, with_grad, *came)
-    came = back(wide_stage, part, with_grad)
-    part = call(wide_back_kernel, [shape((all_rows + rows, half), BF16)], early, with_grad, *came)[0]
+    parts = gathered(rest_back_kernel, narrow_rows, grad, new_w, *pieces)
+    early = [narrow_stage(part, step) for step, part in zip(STEPS, parts)]
+    parts = gathered(narrow_back_kernel, wide_rows, level, parts[X_STEP], *early)
+    came = [wide_stage(part, step) for step, part in zip(STEPS, parts)]
+    part = call(
+        wide_back_kernel, [shape((all_rows + rows, half), BF16)], early[X_STEP], parts[X_STEP], *came,
+    )[0]
     other = to_sibling(part)
     results = [shape((all_rows, width), BF16), shape((rows, width), F32), shape((rows, width), F32)]
     scratch = [pltpu.VMEM((rows, half), F32), pltpu.VMEM((rows, half), F32), pltpu.SemaphoreType.DMA((3,))]

time: 48.9 us -> 45.2 us (0.924)
  starting transfers between devices: 19.1 us -> 16.6 us
  local copies, waits for them, and re-layouts: 0.99 us -> 0.02 us
  waiting for transfers between devices: 22.1 us -> 21.4 us
    ppermute x14 -> x15, starting transfers between devices: 19.1 us -> 16.6 us  [exchange(): return lax.ppermute(value, ('rep', 'shard'), pairs)]
    unnamed x8, local copies, waits for them, and re-layouts: 0.99 us -> 0.02 us
    ppermute x14 -> x15, waiting for transfers between devices: 22.1 us -> 21.4 us  [exchange(): return lax.ppermute(value, ('rep', 'shard'), pairs)]
    pallas_call x10 -> x11, Pallas kernels: 5.89 us -> 6.25 us  [call(): pl.pallas_call(kernel, out_shape=outs, in_specs=[far if i in far_in else...]
  transfers between devices with their start and end apart: 14 -> 15, of which waited for: 11 -> 11; matrix products, arithmetic and copies ran while one was open for 0% -> 0% of each run, Pallas kernels for 3% -> 3%
where the time goes in v2:
time: 45.2 us; the launch traced here: 45.1 us
  waiting for transfers between devices  21.4 us (47%)
  starting transfers between devices  16.6 us (37%)
  Pallas kernels  6.25 us (14%)
  between operations  0.76 us (2%)
    ppermute x15, waiting for transfers between devices, exchange(): return lax.ppermute(value, ('rep', 'shard'), pairs)  21.4 us
    ppermute x15, starting transfers between devices, exchange(): return lax.ppermute(value, ('rep', 'shard'), pairs)  16.6 us
    pallas_call x11, Pallas kernels, call(): pl.pallas_call(kernel, out_shape=outs, in_specs=[far if i in far_in else...  6.25 us
  transfers between devices with their start and end apart: 15, of which 11 were waited for; matrix products, arithmetic and copies ran while one was open for 0% of the time, Pallas kernels for 3%

profile of v2, /device:TPU:0, one launch (start us, length us, event | category | flops | bytes accessed | tf_op | source)
XLA Modules:
  0.0 45.1 jit_solution(16479231298963932763)
XLA Ops:
  0.6 2.9 %shard_map.76 = (bf16[768,2048]{1,0:T(8,128)(2,1)S(1)}, bf16[768,2048]{1,0:T(8,128)(2,1)S(1)}) custom-call(bf16[768,4096]{1,0:T(8,128)(2,1)} %cots_ref.1), custom_call_target="tpu_custom_call" | custom-call | tf_op jit(solution)/shard_map/pallas_call | solution.py:36
  3.6 0.6 %shard_map.77 = (bf16[128,2048]{1,0:T(8,128)(2,1)S(1)}, bf16[128,768]{1,0:T(8,128)(2,1)S(1)}) custom-call(bf16[768,128]{1,0:T(8,128)(2,1)S(1)} %copy-done.2, bf16[768,2048]{1,0:T(8,128)(2,1)S(1)} %get-tuple-element.26.cots), custom_call_target="tpu_custom_call" | custom-call | tf_op jit(solution)/shard_map/pallas_call | solution.py:36
  4.2 0.5 %collective-permute-start = (bf16[128,2048]{1,0:T(8,128)(2,1)S(1)}, bf16[128,2048]{1,0:T(8,128)(2,1)S(1)}, u32[]{:S(2)}, u32[]{:S(2)}) collective-permute-start(bf16[128,2048]{1,0:T(8,128)(2,1)S(1)} %get-tuple-element.29), channel_id=1, source_target_pairs={{0,8},{1,9},{2,10},{3,11},{4,12},{5,13},{6,14},{7,15},{8,0},{9,1},... | collective-permute-start | bytes 1572872 | tf_op jit(solution)/shard_map/ppermute | solution.py:54
  4.7 0.6 %shard_map.78.kept = f32[128,2048]{1,0:T(8,128)S(1)} custom-call(bf16[128,768]{1,0:T(8,128)(2,1)S(1)} %get-tuple-element.27.turned, bf16[768,2048]{1,0:T(8,128)(2,1)S(1)} %get-tuple-element.28.cots), custom_call_target="tpu_custom_call" | custom-call | tf_op jit(solution)/shard_map/pallas_call | solution.py:36
  5.3 0.9 %collective-permute-done.came = bf16[128,2048]{1,0:T(8,128)(2,1)S(1)} collective-permute-done((bf16[128,2048]{1,0:T(8,128)(2,1)S(1)}, bf16[128,2048]{1,0:T(8,128)(2,1)S(1)}, u32[]{:S(2)}, u32[]{:S(2)}) %collective-permute-start) | collective-permute-done | bytes 524320 | tf_op jit(solution)/shard_map/ppermute | solution.py:54
  6.3 3.9 %collective-permute-start.1 = (bf16[64,1024]{1,0:T(8,128)(2,1)S(1)}, bf16[64,1024]{1,0:T(8,128)(2,1)S(1)}, u32[]{:S(2)}, u32[]{:S(2)}) collective-permute-start(bf16[64,1024]{1,0:T(8,128)(2,1)S(1)} %get-tuple-element.31), channel_id=1, source_target_pairs={{0,17},{1,16},{2,19},{3,18},{4,21},{5,20},{6,23},{7,22},{8,14},{9,... | collective-permute-start | bytes 393224 | tf_op jit(solution)/shard_map/ppermute | solution.py:54
  10.2 0.5 %collective-permute-start.2 = (bf16[64,1024]{1,0:T(8,128)(2,1)S(1)}, bf16[64,1024]{1,0:T(8,128)(2,1)S(1)}, u32[]{:S(2)}, u32[]{:S(2)}) collective-permute-start(bf16[64,1024]{1,0:T(8,128)(2,1)S(1)} %get-tuple-element.32), channel_id=1, source_target_pairs={{0,1},{1,0},{2,3},{3,2},{4,5},{5,4},{6,7},{7,6},{8,12},{9,13},{10,... | collective-permute-start | bytes 393224 | tf_op jit(solution)/shard_map/ppermute | solution.py:54
  10.8 2.3 %collective-permute-done.1.refs_0_ = bf16[64,1024]{1,0:T(8,128)(2,1)S(1)} collective-permute-done((bf16[64,1024]{1,0:T(8,128)(2,1)S(1)}, bf16[64,1024]{1,0:T(8,128)(2,1)S(1)}, u32[]{:S(2)}, u32[]{:S(2)}) %collective-permute-start.1) | collective-permute-done | bytes 131104 | tf_op jit(solution)/shard_map/ppermute | solution.py:54
  13.1 2.0 %collective-permute-done.2.refs_1_ = bf16[64,1024]{1,0:T(8,128)(2,1)S(1)} collective-permute-done((bf16[64,1024]{1,0:T(8,128)(2,1)S(1)}, bf16[64,1024]{1,0:T(8,128)(2,1)S(1)}, u32[]{:S(2)}, u32[]{:S(2)}) %collective-permute-start.2) | collective-permute-done | bytes 131104 | tf_op jit(solution)/shard_map/ppermute | solution.py:54
  15.7 3.7 %collective-permute-start.4 = (bf16[16,1024]{1,0:T(8,128)(2,1)S(1)}, bf16[16,1024]{1,0:T(8,128)(2,1)S(1)}, u32[]{:S(2)}, u32[]{:S(2)}) collective-permute-start(bf16[16,1024]{1,0:T(8,128)(2,1)S(1)} %get-tuple-element.35), channel_id=1, source_target_pairs={{0,6},{1,7},{2,4},{3,5},{4,2},{5,3},{6,0},{7,1},{8,25},{9,24},{10,... | collective-permute-start | bytes 98312 | tf_op jit(solution)/shard_map/ppermute | solution.py:54
  19.4 0.8 %collective-permute-start.6 = (bf16[16,1024]{1,0:T(8,128)(2,1)S(1)}, bf16[16,1024]{1,0:T(8,128)(2,1)S(1)}, u32[]{:S(2)}, u32[]{:S(2)}) collective-permute-start(bf16[16,1024]{1,0:T(8,128)(2,1)S(1)} %get-tuple-element.37), channel_id=1, source_target_pairs={{0,2},{1,3},{2,0},{3,1},{4,6},{5,7},{6,4},{7,5},{8,24},{9,25},{10,... | collective-permute-start | bytes 98312 | tf_op jit(solution)/shard_map/ppermute | solution.py:54
  20.2 1.3 %collective-permute-done.4.refs_0_ = bf16[16,1024]{1,0:T(8,128)(2,1)S(1)} collective-permute-done((bf16[16,1024]{1,0:T(8,128)(2,1)S(1)}, bf16[16,1024]{1,0:T(8,128)(2,1)S(1)}, u32[]{:S(2)}, u32[]{:S(2)}) %collective-permute-start.4) | collective-permute-done | bytes 32800 | tf_op jit(solution)/shard_map/ppermute | solution.py:54
  21.5 2.7 %collective-permute-done.5.refs_1_ = bf16[16,1024]{1,0:T(8,128)(2,1)S(1)} collective-permute-done((bf16[16,1024]{1,0:T(8,128)(2,1)S(1)}, bf16[16,1024]{1,0:T(8,128)(2,1)S(1)}, u32[]{:S(2)}, u32[]{:S(2)}) %collective-permute-start.5) | collective-permute-done | bytes 32800 | tf_op jit(solution)/shard_map/ppermute | solution.py:54
  24.5 3.4 %collective-permute-start.9 = (bf16[16,1024]{1,0:T(8,128)(2,1)S(1)}, bf16[16,1024]{1,0:T(8,128)(2,1)S(1)}, u32[]{:S(2)}, u32[]{:S(2)}) collective-permute-start(bf16[16,1024]{1,0:T(8,128)(2,1)S(1)} %get-tuple-element.41), channel_id=1, source_target_pairs={{0,6},{1,7},{2,4},{3,5},{4,2},{5,3},{6,0},{7,1},{8,25},{9,24},{10,... | collective-permute-start | bytes 98312 | tf_op jit(solution)/shard_map/ppermute | solution.py:54
  27.9 2.6 %collective-permute-done.9.refs_0_ = bf16[16,1024]{1,0:T(8,128)(2,1)S(1)} collective-permute-done((bf16[16,1024]{1,0:T(8,128)(2,1)S(1)}, bf16[16,1024]{1,0:T(8,128)(2,1)S(1)}, u32[]{:S(2)}, u32[]{:S(2)}) %collective-permute-start.9) | collective-permute-done | bytes 32800 | tf_op jit(solution)/shard_map/ppermute | solution.py:54
  30.5 2.3 %collective-permute-done.10.refs_1_ = bf16[16,1024]{1,0:T(8,128)(2,1)S(1)} collective-permute-done((bf16[16,1024]{1,0:T(8,128)(2,1)S(1)}, bf16[16,1024]{1,0:T(8,128)(2,1)S(1)}, u32[]{:S(2)}, u32[]{:S(2)}) %collective-permute-start.10) | collective-permute-done | bytes 32800 | tf_op jit(solution)/shard_map/ppermute | solution.py:54
  32.9 0.9 %collective-permute-start.13 = (bf16[80,1024]{1,0:T(8,128)(2,1)S(1)}, bf16[80,1024]{1,0:T(8,128)(2,1)S(1)}, u32[]{:S(2)}, u32[]{:S(2)}) collective-permute-start(bf16[80,1024]{1,0:T(8,128)(2,1)S(1)} %get-tuple-element.43.own), channel_id=1, source_target_pairs={{0,16},{1,17},{2,18},{3,19},{4,20},{5,21},{6,22},{7,23},{8,10},{9,... | collective-permute-start | bytes 491528 | tf_op jit(solution)/shard_map/ppermute | solution.py:54
  33.8 2.1 %collective-permute-start.11 = (bf16[64,1024]{1,0:T(8,128)(2,1)S(1)}, bf16[64,1024]{1,0:T(8,128)(2,1)S(1)}, u32[]{:S(2)}, u32[]{:S(2)}) collective-permute-start(bf16[64,1024]{1,0:T(8,128)(2,1)S(1)} %get-tuple-element.44), channel_id=1, source_target_pairs={{0,17},{1,16},{2,19},{3,18},{4,21},{5,20},{6,23},{7,22},{8,14},{9,... | collective-permute-start | bytes 393224 | tf_op jit(solution)/shard_map/ppermute | solution.py:54
  35.9 0.5 %collective-permute-start.12 = (bf16[64,1024]{1,0:T(8,128)(2,1)S(1)}, bf16[64,1024]{1,0:T(8,128)(2,1)S(1)}, u32[]{:S(2)}, u32[]{:S(2)}) collective-permute-start(bf16[64,1024]{1,0:T(8,128)(2,1)S(1)} %get-tuple-element.45), channel_id=1, source_target_pairs={{0,1},{1,0},{2,3},{3,2},{4,5},{5,4},{6,7},{7,6},{8,12},{9,13},{10,... | collective-permute-start | bytes 393224 | tf_op jit(solution)/shard_map/ppermute | solution.py:54
  36.4 4.3 %collective-permute-done.11.refs_0_ = bf16[64,1024]{1,0:T(8,128)(2,1)S(1)} collective-permute-done((bf16[64,1024]{1,0:T(8,128)(2,1)S(1)}, bf16[64,1024]{1,0:T(8,128)(2,1)S(1)}, u32[]{:S(2)}, u32[]{:S(2)}) %collective-permute-start.11) | collective-permute-done | bytes 131104 | tf_op jit(solution)/shard_map/ppermute | solution.py:54
  40.7 1.3 %collective-permute-done.12.refs_1_ = bf16[64,1024]{1,0:T(8,128)(2,1)S(1)} collective-permute-done((bf16[64,1024]{1,0:T(8,128)(2,1)S(1)}, bf16[64,1024]{1,0:T(8,128)(2,1)S(1)}, u32[]{:S(2)}, u32[]{:S(2)}) %collective-permute-start.12) | collective-permute-done | bytes 131104 | tf_op jit(solution)/shard_map/ppermute | solution.py:54
  42.2 0.9 %shard_map.85 = (bf16[128,4096]{1,0:T(8,128)(2,1)}, f32[16,4096]{1,0:T(8,128)}, f32[16,4096]{1,0:T(8,128)}) custom-call(bf16[144,2048]{1,0:T(8,128)(2,1)S(1)} %shard_map.84.part, f32[16,4096]{1,0:T(8,128)S(1)} %copy-done, f32[16,4096]{1,0:T(8,128)S(1)} %copy-done.1), custom_call_target="tpu_custom_call" | custom-call | tf_op jit(solution)/shard_map/pallas_call | solution.py:36
  43.1 1.1 %collective-permute-done.14.part = bf16[144,2048]{1,0:T(8,128)(2,1)S(1)} collective-permute-done((bf16[144,2048]{1,0:T(8,128)(2,1)S(1)}, bf16[144,2048]{1,0:T(8,128)(2,1)S(1)}, u32[]{:S(2)}, u32[]{:S(2)}) %collective-permute-start.14) | collective-permute-done | bytes 589856 | tf_op jit(solution)/shard_map/ppermute | solution.py:54
  44.2 0.9 %shard_map.86 = (bf16[128,4096]{1,0:T(8,128)(2,1)}, f32[16,4096]{1,0:T(8,128)}, f32[16,4096]{1,0:T(8,128)}) custom-call(bf16[144,2048]{1,0:T(8,128)(2,1)S(1)} %collective-permute-done.14.part, f32[16,4096]{1,0:T(8,128)S(1)} %copy-done, f32[16,4096]{1,0:T(8,128)S(1)} %copy-done.1, ...), custom_call_target="tpu_custom_call", output_to_operand_aliasing={{0}: (3, {}), {1}: (4, {}), {2}: (5, {})} | custom-call | tf_op jit(solution)/shard_map/pallas_call | solution.py:36
  (25 shorter events, 1.2 us)
Async XLA Ops:
  0.6 2.9 %copy-start.2 = (bf16[768,128]{1,0:T(8,128)(2,1)S(1)}, bf16[768,128]{1,0:T(8,128)(2,1)}, u32[]{:S(2)}) copy-start(bf16[768,128]{1,0:T(8,128)(2,1)} %acts.1) | copy-start | bytes 589828
  4.2 2.0 %collective-permute-start = (bf16[128,2048]{1,0:T(8,128)(2,1)S(1)}, bf16[128,2048]{1,0:T(8,128)(2,1)S(1)}, u32[]{:S(2)}, u32[]{:S(2)}) collective-permute-start(bf16[128,2048]{1,0:T(8,128)(2,1)S(1)} %get-tuple-element.29), channel_id=1, source_target_pairs={{0,8},{1,9},{2,10},{3,11},{4,12},{5,13},{6,14},{7,15},{8,0},{9,1},... | collective-permute-start | bytes 1572872 | tf_op jit(solution)/shard_map/ppermute | solution.py:54
  4.7 19.5 %copy-start = (f32[16,4096]{1,0:T(8,128)S(1)}, f32[16,4096]{1,0:T(8,128)}, u32[]{:S(2)}) copy-start(f32[16,4096]{1,0:T(8,128)} %m.5) | copy-start | bytes 786436
  4.7 19.5 %copy-start.1 = (f32[16,4096]{1,0:T(8,128)S(1)}, f32[16,4096]{1,0:T(8,128)}, u32[]{:S(2)}) copy-start(f32[16,4096]{1,0:T(8,128)} %v.5) | copy-start | bytes 786436
  4.7 19.5 %copy-start.3 = (bf16[16,4096]{1,0:T(8,128)(2,1)S(1)}, bf16[16,4096]{1,0:T(8,128)(2,1)}, u32[]{:S(2)}) copy-start(bf16[16,4096]{1,0:T(8,128)(2,1)} %w.1) | copy-start | bytes 393220
  6.3 6.8 %collective-permute-start.1 = (bf16[64,1024]{1,0:T(8,128)(2,1)S(1)}, bf16[64,1024]{1,0:T(8,128)(2,1)S(1)}, u32[]{:S(2)}, u32[]{:S(2)}) collective-permute-start(bf16[64,1024]{1,0:T(8,128)(2,1)S(1)} %get-tuple-element.31), channel_id=1, source_target_pairs={{0,17},{1,16},{2,19},{3,18},{4,21},{5,20},{6,23},{7,22},{8,14},{9,... | collective-permute-start | bytes 393224 | tf_op jit(solution)/shard_map/ppermute | solution.py:54
  10.2 5.0 %collective-permute-start.2 = (bf16[64,1024]{1,0:T(8,128)(2,1)S(1)}, bf16[64,1024]{1,0:T(8,128)(2,1)S(1)}, u32[]{:S(2)}, u32[]{:S(2)}) collective-permute-start(bf16[64,1024]{1,0:T(8,128)(2,1)S(1)} %get-tuple-element.32), channel_id=1, source_target_pairs={{0,1},{1,0},{2,3},{3,2},{4,5},{5,4},{6,7},{7,6},{8,12},{9,13},{10,... | collective-permute-start | bytes 393224 | tf_op jit(solution)/shard_map/ppermute | solution.py:54
  10.7 5.0 %collective-permute-start.3 = (bf16[64,1024]{1,0:T(8,128)(2,1)S(1)}, bf16[64,1024]{1,0:T(8,128)(2,1)S(1)}, u32[]{:S(2)}, u32[]{:S(2)}) collective-permute-start(bf16[64,1024]{1,0:T(8,128)(2,1)S(1)} %get-tuple-element.33), channel_id=1, source_target_pairs={{0,16},{1,17},{2,18},{3,19},{4,20},{5,21},{6,22},{7,23},{8,10},{9,... | collective-permute-start | bytes 393224 | tf_op jit(solution)/shard_map/ppermute | solution.py:54
  15.7 5.8 %collective-permute-start.4 = (bf16[16,1024]{1,0:T(8,128)(2,1)S(1)}, bf16[16,1024]{1,0:T(8,128)(2,1)S(1)}, u32[]{:S(2)}, u32[]{:S(2)}) collective-permute-start(bf16[16,1024]{1,0:T(8,128)(2,1)S(1)} %get-tuple-element.35), channel_id=1, source_target_pairs={{0,6},{1,7},{2,4},{3,5},{4,2},{5,3},{6,0},{7,1},{8,25},{9,24},{10,... | collective-permute-start | bytes 98312 | tf_op jit(solution)/shard_map/ppermute | solution.py:54
  19.4 4.8 %collective-permute-start.5 = (bf16[16,1024]{1,0:T(8,128)(2,1)S(1)}, bf16[16,1024]{1,0:T(8,128)(2,1)S(1)}, u32[]{:S(2)}, u32[]{:S(2)}) collective-permute-start(bf16[16,1024]{1,0:T(8,128)(2,1)S(1)} %get-tuple-element.36), channel_id=1, source_target_pairs={{0,4},{1,5},{2,6},{3,7},{4,0},{5,1},{6,2},{7,3},{8,9},{9,8},{10,11... | collective-permute-start | bytes 98312 | tf_op jit(solution)/shard_map/ppermute | solution.py:54
  19.4 4.8 %collective-permute-start.6 = (bf16[16,1024]{1,0:T(8,128)(2,1)S(1)}, bf16[16,1024]{1,0:T(8,128)(2,1)S(1)}, u32[]{:S(2)}, u32[]{:S(2)}) collective-permute-start(bf16[16,1024]{1,0:T(8,128)(2,1)S(1)} %get-tuple-element.37), channel_id=1, source_target_pairs={{0,2},{1,3},{2,0},{3,1},{4,6},{5,7},{6,4},{7,5},{8,24},{9,25},{10,... | collective-permute-start | bytes 98312 | tf_op jit(solution)/shard_map/ppermute | solution.py:54
  24.4 8.5 %collective-permute-start.7 = (bf16[32,1024]{1,0:T(8,128)(2,1)S(1)}, bf16[32,1024]{1,0:T(8,128)(2,1)S(1)}, u32[]{:S(2)}, u32[]{:S(2)}) collective-permute-start(bf16[32,1024]{1,0:T(8,128)(2,1)S(1)} %get-tuple-element.40.own), channel_id=1, source_target_pairs={{0,2},{1,3},{2,0},{3,1},{4,6},{5,7},{6,4},{7,5},{8,24},{9,25},{10,... | collective-permute-start | bytes 196616 | tf_op jit(solution)/shard_map/ppermute | solution.py:54
  24.4 3.5 %collective-permute-start.8 = (bf16[16,1024]{1,0:T(8,128)(2,1)S(1)}, bf16[16,1024]{1,0:T(8,128)(2,1)S(1)}, u32[]{:S(2)}, u32[]{:S(2)}) collective-permute-start(bf16[16,1024]{1,0:T(8,128)(2,1)S(1)} %get-tuple-element.38.grad), channel_id=1, source_target_pairs={{0,8},{1,9},{2,10},{3,11},{4,12},{5,13},{6,14},{7,15},{8,0},{9,1},... | collective-permute-start | bytes 98312 | tf_op jit(solution)/shard_map/ppermute | solution.py:54
  24.5 6.0 %collective-permute-start.9 = (bf16[16,1024]{1,0:T(8,128)(2,1)S(1)}, bf16[16,1024]{1,0:T(8,128)(2,1)S(1)}, u32[]{:S(2)}, u32[]{:S(2)}) collective-permute-start(bf16[16,1024]{1,0:T(8,128)(2,1)S(1)} %get-tuple-element.41), channel_id=1, source_target_pairs={{0,6},{1,7},{2,4},{3,5},{4,2},{5,3},{6,0},{7,1},{8,25},{9,24},{10,... | collective-permute-start | bytes 98312 | tf_op jit(solution)/shard_map/ppermute | solution.py:54
  27.9 4.9 %collective-permute-start.10 = (bf16[16,1024]{1,0:T(8,128)(2,1)S(1)}, bf16[16,1024]{1,0:T(8,128)(2,1)S(1)}, u32[]{:S(2)}, u32[]{:S(2)}) collective-permute-start(bf16[16,1024]{1,0:T(8,128)(2,1)S(1)} %get-tuple-element.42), channel_id=1, source_target_pairs={{0,4},{1,5},{2,6},{3,7},{4,0},{5,1},{6,2},{7,3},{8,9},{9,8},{10,11... | collective-permute-start | bytes 98312 | tf_op jit(solution)/shard_map/ppermute | solution.py:54
  32.9 9.1 %collective-permute-start.13 = (bf16[80,1024]{1,0:T(8,128)(2,1)S(1)}, bf16[80,1024]{1,0:T(8,128)(2,1)S(1)}, u32[]{:S(2)}, u32[]{:S(2)}) collective-permute-start(bf16[80,1024]{1,0:T(8,128)(2,1)S(1)} %get-tuple-element.43.own), channel_id=1, source_target_pairs={{0,16},{1,17},{2,18},{3,19},{4,20},{5,21},{6,22},{7,23},{8,10},{9,... | collective-permute-start | bytes 491528 | tf_op jit(solution)/shard_map/ppermute | solution.py:54
  33.8 6.9 %collective-permute-start.11 = (bf16[64,1024]{1,0:T(8,128)(2,1)S(1)}, bf16[64,1024]{1,0:T(8,128)(2,1)S(1)}, u32[]{:S(2)}, u32[]{:S(2)}) collective-permute-start(bf16[64,1024]{1,0:T(8,128)(2,1)S(1)} %get-tuple-element.44), channel_id=1, source_target_pairs={{0,17},{1,16},{2,19},{3,18},{4,21},{5,20},{6,23},{7,22},{8,14},{9,... | collective-permute-start | bytes 393224 | tf_op jit(solution)/shard_map/ppermute | solution.py:54
  35.9 6.1 %collective-permute-start.12 = (bf16[64,1024]{1,0:T(8,128)(2,1)S(1)}, bf16[64,1024]{1,0:T(8,128)(2,1)S(1)}, u32[]{:S(2)}, u32[]{:S(2)}) collective-permute-start(bf16[64,1024]{1,0:T(8,128)(2,1)S(1)} %get-tuple-element.45), channel_id=1, source_target_pairs={{0,1},{1,0},{2,3},{3,2},{4,5},{5,4},{6,7},{7,6},{8,12},{9,13},{10,... | collective-permute-start | bytes 393224 | tf_op jit(solution)/shard_map/ppermute | solution.py:54
  42.1 2.1 %collective-permute-start.14 = (bf16[144,2048]{1,0:T(8,128)(2,1)S(1)}, bf16[144,2048]{1,0:T(8,128)(2,1)S(1)}, u32[]{:S(2)}, u32[]{:S(2)}) collective-permute-start(bf16[144,2048]{1,0:T(8,128)(2,1)S(1)} %shard_map.84.part), channel_id=1, source_target_pairs={{0,8},{1,9},{2,10},{3,11},{4,12},{5,13},{6,14},{7,15},{8,0},{9,1},... | collective-permute-start | bytes 1769480 | tf_op jit(solution)/shard_map/ppermute | solution.py:54
